TPU v7x, 128 devices: a whole 4x4x4 slice. The times are simulated.
128 devices in a mesh: seq: 32 (over y, x, core), ch: 4 (over z).
Axes of the slice: x: 4, y: 4, z: 4, core: 2. Of those that a mesh axis runs over, the one named last changes fastest.
Arguments:
- tokens: bfloat16 [16384, 4096], P('seq', 'ch'), may hold values from -6 to 6
- w_in: bfloat16 [4096, 3, 2048], P(None, None, 'ch'), may hold values from -0.09375 to 0.09375
- w_out: bfloat16 [2048, 4096], P('ch'), may hold values from -0.125 to 0.125
- spectra: float32 [2, 64, 512, 2048], P(None, 'seq', None, 'ch'), may hold values from -8 to 8
Outputs:
- mixed_out: bfloat16 [16384, 4096], P('seq', 'ch')
All inputs are finite; a program needn't handle non-finite values.
Results may differ from a plain program's by a relative error of at most 0.007.
Values may be sent and summed in bfloat16 or wider, within the bound.
A program may use at most 128 MiB of HBM per device.

v0:
```python
import math

import jax
import jax.numpy as jnp
from jax import lax
from jax.sharding import PartitionSpec as P

exact_mode = lax.Precision.HIGHEST


def angles(first_idx, second_idx, modulus):
    index_prod = first_idx[:, None] * second_idx[None, :] % modulus
    phase = 2.0 * math.pi / modulus * index_prod.astype(jnp.float32)
    return (jnp.cos(phase), jnp.sin(phase))


def apply_rows(matrix, values_in):
    return jnp.einsum("kb,rbc->rkc", matrix, values_in, precision=exact_mode)


def forward_outer(incoming, device_pos, total_len):
    count_p = incoming.shape[0]
    per_dev = incoming.shape[1]
    freq_a = jnp.arange(2 * count_p, dtype=jnp.int32)
    cos_table, sine_table = angles(freq_a, jnp.arange(count_p, dtype=jnp.int32), 2 * count_p)
    real_part = jnp.einsum("kp,pbc->kbc", cos_table, incoming, precision=exact_mode)
    imag_part = -jnp.einsum("kp,pbc->kbc", sine_table, incoming, precision=exact_mode)
    global_pos = device_pos * per_dev + jnp.arange(per_dev, dtype=jnp.int32)
    twist_cos, twist_sin = angles(freq_a, global_pos, total_len)
    twist_cos = twist_cos[:, :, None]
    twist_sin = twist_sin[:, :, None]
    new_real = real_part * twist_cos + imag_part * twist_sin
    new_imag = imag_part * twist_cos - real_part * twist_sin
    return jnp.stack([new_real, new_imag])


def forward_inner(incoming):
    width_b = incoming.shape[2]
    positions = jnp.arange(width_b, dtype=jnp.int32)
    cos_table, sine_table = angles(positions, positions, width_b)
    real_part = incoming[0]
    imag_part = incoming[1]
    real_out = apply_rows(cos_table, real_part) + apply_rows(sine_table, imag_part)
    imag_out = apply_rows(cos_table, imag_part) - apply_rows(sine_table, real_part)
    return jnp.stack([real_out, imag_out])


def local(tokens, w_in, w_out, spectra):
    features_all = lax.all_gather(tokens, "ch", axis=1, tiled=True)
    projected = jnp.einsum(
        "td,dgc->gtc", features_all, w_in, preferred_element_type=jnp.float32
    ).astype(jnp.bfloat16)
    query_rows = projected[0]
    signal = projected[1].astype(jnp.float32) * projected[2].astype(jnp.float32)
    seq_count = lax.axis_size("seq")
    device_pos = lax.axis_index("seq")
    tok_local = signal.shape[0]
    total_len = 2 * seq_count * tok_local
    stacked = signal[None]
    moved_rows = lax.all_to_all(stacked, "seq", split_axis=1, concat_axis=0, tiled=True)
    outer_part = forward_outer(moved_rows, device_pos, total_len)
    regrouped = lax.all_to_all(outer_part, "seq", split_axis=1, concat_axis=2, tiled=True)
    spectrum = forward_inner(regrouped)
    prod_real = spectra[0] * spectrum[0] - spectra[1] * spectrum[1]
    prod_imag = spectra[0] * spectrum[1] + spectra[1] * spectrum[0]
    positions = jnp.arange(tok_local, dtype=jnp.int32)
    cos_table, sine_table = angles(positions, positions, tok_local)
    back_real = apply_rows(cos_table, prod_real) - apply_rows(sine_table, prod_imag)
    back_imag = apply_rows(cos_table, prod_imag) + apply_rows(sine_table, prod_real)
    freq_own = 2 * device_pos + jnp.arange(2, dtype=jnp.int32)
    twist_cos, twist_sin = angles(freq_own, positions, total_len)
    twist_cos = twist_cos[:, :, None]
    twist_sin = twist_sin[:, :, None]
    turned = jnp.stack(
        [
            back_real * twist_cos - back_imag * twist_sin,
            back_imag * twist_cos + back_real * twist_sin,
        ]
    )
    spread_out = lax.all_to_all(turned, "seq", split_axis=2, concat_axis=1, tiled=True)
    outer_cos, outer_sin = angles(
        jnp.arange(seq_count, dtype=jnp.int32),
        jnp.arange(2 * seq_count, dtype=jnp.int32),
        2 * seq_count,
    )
    partial_conv = (
        jnp.einsum("pk,kbc->pbc", outer_cos, spread_out[0], precision=exact_mode)
        - jnp.einsum("pk,kbc->pbc", outer_sin, spread_out[1], precision=exact_mode)
    ) * (1.0 / total_len)
    convolved = lax.all_to_all(partial_conv, "seq", split_axis=0, concat_axis=1, tiled=True)[0]
    gated_rows = (query_rows.astype(jnp.float32) * convolved).astype(jnp.bfloat16)
    partial_out = jnp.dot(gated_rows, w_out, preferred_element_type=jnp.float32)
    mixed_out = lax.psum_scatter(partial_out, "ch", scatter_dimension=1, tiled=True).astype(
        jnp.bfloat16
    )
    return mixed_out


def solution(mesh):
    in_specs = (P("seq", "ch"), P(None, None, "ch"), P("ch", None), P(None, "seq", None, "ch"))
    out_specs = P("seq", "ch")
    return jax.shard_map(local, mesh=mesh, in_specs=in_specs, out_specs=out_specs, check_vma=False)
```

profile of v0, /device:TPU:1, one launch (start us, length us, event | category | flops | bytes accessed | tf_op | source)
XLA Modules:
  0.0 452.6 jit_solution(10764409712691111225)
XLA Ops:
  7.3 53.5 %all-gather.2.cloned.1.call-done = bf16[512,4096]{1,0:T(8,128)(2,1)} async-done(((bf16[512,1024]{1,0:T(8,128)(2,1)}), bf16[512,4096]{1,0:T(8,128)(2,1)}) %all-gather.2.cloned.1.call-update) | async-done | bytes 4194320 | tf_op jit(solution)/shard_map/all_gather | solution.py:49
  60.7 11.0 %fusion.7 = bf16[3,512,512]{1,2,0:T(8,128)(2,1)S(1)} fusion(bf16[4096,3,512]{2,0,1:T(8,128)(2,1)} %param.5, bf16[512,4096]{1,0:T(8,128)(2,1)} %all-gather.2.cloned.1.call-done), kind=kOutput, calls=%fused_computation.22 | convolution fusion | flops 6443237376 | bytes 18350080 | tf_op jit(solution)/shard_map/td,dgc->gtc/dot_general | solution.py:50
  75.0 7.9 %all-to-all-start = ((f32[1,512,512]{2,0,1:T(1,128)}), f32[1,512,512]{2,0,1:T(1,128)S(1)}, u32[]{:S(2)}, u32[]{:S(2)}) async-start(f32[1,512,512]{2,0,1:T(1,128)} %copy.50), calls=%async_computation | async-start | bytes 2097152 | tf_op jit(solution)/shard_map/all_to_all | solution.py:60
  83.0 16.9 %all-to-all-done = f32[1,512,512]{2,0,1:T(1,128)S(1)} async-done(((f32[1,512,512]{2,0,1:T(1,128)}), f32[1,512,512]{2,0,1:T(1,128)S(1)}, u32[]{:S(2)}, u32[]{:S(2)}) %all-to-all-start) | async-done | bytes 1048608 | tf_op jit(solution)/shard_map/all_to_all | solution.py:60
  106.0 4.4 copy.53
  110.4 4.9 %all-to-all-start.1 = ((f32[2,64,16,512]{3,2,0,1:T(8,128)}), f32[2,64,16,512]{3,2,0,1:T(8,128)}, u32[]{:S(2)}, u32[]{:S(2)}) async-start(f32[2,64,16,512]{3,2,0,1:T(8,128)} %copy.53), calls=%async_computation.1 | async-start | bytes 8388608 | tf_op jit(solution)/shard_map/all_to_all | solution.py:62
  115.7 4.6 %fusion.133 = (f32[1,2,512,512]{3,2,1,0:T(8,128)}, f32[1,2,512,512]{3,2,1,0:T(8,128)}) fusion(f32[2,2,512,512]{3,2,1,0:T(8,128)} %param.7), kind=kLoop, calls=%fused_computation.151 | loop fusion | bytes 8388608 | tf_op jit(solution)/shard_map/slice | solution.py:64
  122.2 3.0 copy.75
  125.4 40.3 %all-to-all-done.1 = f32[2,64,16,512]{3,2,0,1:T(8,128)} async-done(((f32[2,64,16,512]{3,2,0,1:T(8,128)}), f32[2,64,16,512]{3,2,0,1:T(8,128)}, u32[]{:S(2)}, u32[]{:S(2)}) %all-to-all-start.1) | async-done | bytes 4194336 | tf_op jit(solution)/shard_map/all_to_all | solution.py:62
  169.5 10.8 %fusion.25 = f32[2,512,512]{2,1,0:T(8,128)S(1)} fusion(f32[2,512,512]{2,1,0:T(8,128)S(1)} %bitcast.113), kind=kOutput, calls=%fused_computation.40 | convolution fusion | flops 3224895488 | bytes 4194304 | tf_op jit(solution)/shard_map/kb,rbc->rkc/dot_general | solution.py:18
  180.5 11.5 %fusion.23 = f32[2,512,512]{2,1,0:T(8,128)S(1)} fusion(f32[2,512,512]{2,1,0:T(8,128)S(1)} %bitcast.115), kind=kOutput, calls=%fused_computation.38 | convolution fusion | flops 3224895488 | bytes 4194304 | tf_op jit(solution)/shard_map/kb,rbc->rkc/dot_general | solution.py:18
  192.0 11.2 %convolution_add_fusion.1 = f32[2,512,512]{2,1,0:T(8,128)S(1)} fusion(f32[2,512,512]{2,1,0:T(8,128)S(1)} %fusion.25, f32[2,512,512]{2,1,0:T(8,128)S(1)} %bitcast.116), kind=kOutput, calls=%fused_computation.18 | convolution fusion | flops 3225419776 | bytes 6291456 | tf_op jit(solution)/shard_map/kb,rbc->rkc/dot_general | solution.py:18
  203.2 11.8 %fusion.3 = (f32[2,512,512]{1,2,0:T(8,128)S(1)}, f32[2,512,512]{1,2,0:T(8,128)S(1)}) fusion(f32[1,2,512,512]{2,3,1,0:T(8,128)S(1)} %copy-done, f32[2,512,512]{2,1,0:T(8,128)S(1)} %convolution_add_fusion.1, f32[1,2,512,512]{2,3,1,0:T(8,128)S(1)} %copy.74, f32[2,512,512]{2,1,0:T(8,128)S(1)} %fusion.23, f32[2,512,512]{2,1,0:T(8,128)S(1)} %bitcast.114), kind=kOutput, calls=%fused_computation.7 | convolution fusion | flops 3228565504 | bytes 14680064 | tf_op jit(solution)/shard_map/kb,rbc->rkc/dot_general | solution.py:18
  215.1 8.4 %fusion.19 = f32[2,512,512]{2,1,0:T(8,128)S(1)} fusion(f32[2,512,512]{1,2,0:T(8,128)S(1)} %get-tuple-element.5), kind=kOutput, calls=%fused_computation.34 | convolution fusion | flops 3224895488 | bytes 4194304 | tf_op jit(solution)/shard_map/kb,rbc->rkc/dot_general | solution.py:18
  223.5 8.6 %fusion.21 = f32[2,512,512]{2,1,0:T(8,128)S(1)} fusion(f32[2,512,512]{1,2,0:T(8,128)S(1)} %get-tuple-element.6), kind=kOutput, calls=%fused_computation.36 | convolution fusion | flops 3224895488 | bytes 4194304 | tf_op jit(solution)/shard_map/kb,rbc->rkc/dot_general | solution.py:18
  232.1 8.5 %convolution_add_fusion = f32[2,512,512]{2,1,0:T(8,128)S(1)} fusion(f32[2,512,512]{2,1,0:T(8,128)S(1)} %fusion.19, f32[2,512,512]{1,2,0:T(8,128)S(1)} %get-tuple-element.6), kind=kOutput, calls=%fused_computation.15 | convolution fusion | flops 3225419776 | bytes 6291456 | tf_op jit(solution)/shard_map/kb,rbc->rkc/dot_general | solution.py:18
  240.6 8.7 %subtract_bitcast_fusion = (f32[1,2,512,512]{2,3,1,0:T(8,128)S(1)}, f32[1,2,512,512]{2,3,1,0:T(8,128)S(1)}) fusion(f32[2,512,512]{2,1,0:T(8,128)S(1)} %convolution_add_fusion, f32[2,512]{1,0:T(2,128)S(1)} %get-tuple-element.18, f32[2,512]{1,0:T(2,128)S(1)} %get-tuple-element.17, f32[2,512,512]{2,1,0:T(8,128)S(1)} %fusion.21, ...), kind=kOutput, calls=%fused_computation.11 | convolution fusion | flops 3228565504 | bytes 10493952 | tf_op jit(solution)/shard_map/kb,rbc->rkc/dot_general | solution.py:18
  251.7 7.3 %copy.62 = f32[2,2,512,512]{3,1,0,2:T(2,128)} copy(f32[2,2,512,512]{2,3,1,0:T(8,128)} %pad_maximum_fusion.1) | data formatting | bytes 8388608 | tf_op jit(solution)/shard_map/stack | solution.py:74
  259.0 58.6 %all_to_all.51 = f32[2,2,512,512]{3,1,0,2:T(2,128)S(1)} all-to-all(f32[2,2,512,512]{3,1,0,2:T(2,128)} %copy.62), channel_id=1, replica_groups=mesh['seq'=32,'ch'=4] {'seq'}, dimensions={2} | all-to-all | bytes 8388608 | tf_op jit(solution)/shard_map/all_to_all | solution.py:80
  325.1 2.9 fusion.55
  328.1 3.0 copy.65
  335.5 21.5 %all_to_all.52 = f32[32,16,512]{2,1,0:T(8,128)S(1)} all-to-all(f32[32,16,512]{2,1,0:T(8,128)S(1)} %copy.66), channel_id=1, replica_groups=mesh['seq'=32,'ch'=4] {'seq'}, dimensions={0} | all-to-all | bytes 2097152 | tf_op jit(solution)/shard_map/all_to_all | solution.py:90
  357.4 8.0 %fusion.34 = f32[512,4096]{1,0:T(8,128)} fusion(bf16[512,4096]{1,0:T(8,128)(2,1)} %param.6, f32[512,512]{0,1:T(8,128)S(1)} %copy.67, bf16[3,512,512]{1,2,0:T(8,128)(2,1)} %copy-done.2), kind=kOutput, calls=%fused_computation.50 | convolution fusion | flops 2148270080 | bytes 14155776 | tf_op jit(solution)/shard_map/dot_general | solution.py:92
  365.4 77.4 %reduce-scatter.2.cloned.1.call-done = f32[512,1024]{1,0:T(8,128)} async-done(((f32[512,4096]{1,0:T(8,128)}), f32[512,1024]{1,0:T(8,128)}) %reduce-scatter.2.cloned.1.call-update) | async-done | bytes 2097168 | tf_op jit(solution)/shard_map/reduce_scatter | solution.py:93
  (35 shorter events, 33.9 us)
Async XLA Ops:
  6.5 54.2 %all-gather.2.cloned.1.call-start = ((), (), s32[]{:S(2)}) async-start(), calls=%async_computation.5 | async-start | bytes 5242880 | tf_op jit(solution)/shard_map/all_gather | solution.py:49
  71.7 1.2 copy-start.2
  75.0 25.0 %all-to-all-start = ((f32[1,512,512]{2,0,1:T(1,128)}), f32[1,512,512]{2,0,1:T(1,128)S(1)}, u32[]{:S(2)}, u32[]{:S(2)}) async-start(f32[1,512,512]{2,0,1:T(1,128)} %copy.50), calls=%async_computation | async-start | bytes 2097152 | tf_op jit(solution)/shard_map/all_to_all | solution.py:60
  110.4 55.2 %all-to-all-start.1 = ((f32[2,64,16,512]{3,2,0,1:T(8,128)}), f32[2,64,16,512]{3,2,0,1:T(8,128)}, u32[]{:S(2)}, u32[]{:S(2)}) async-start(f32[2,64,16,512]{3,2,0,1:T(8,128)} %copy.53), calls=%async_computation.1 | async-start | bytes 8388608 | tf_op jit(solution)/shard_map/all_to_all | solution.py:62
  115.3 327.5 %reduce-scatter.2.cloned.1.call-start = ((), (), s32[]{:S(2)}) async-start(), calls=%async_computation.6 | async-start | bytes 10485760 | tf_op jit(solution)/shard_map/reduce_scatter | solution.py:93
  192.0 11.2 %copy-start = (f32[1,2,512,512]{2,3,1,0:T(8,128)S(1)}, f32[1,2,512,512]{2,3,1,0:T(8,128)}, u32[]{:S(2)}) copy-start(f32[1,2,512,512]{2,3,1,0:T(8,128)} %copy.75) | copy-start | bytes 6291460
  325.1 2.9 copy-start.1
Sparse Core Ops, SparseCore 0:
  9.0 51.6 all-gather.1
  365.6 77.2 reduce-scatter.1
where the time goes:
time: 457 us; the launch traced here: 453 us
  waiting for transfers between devices  189 us (41%)
  matrix products  108 us (24%)
  blocking collectives  80.2 us (18%)
  local copies, waits for them, and re-layouts  42.4 us (9%)
  between operations  13.9 us (3%)
  starting transfers between devices  13.2 us (3%)
  other arithmetic  6.26 us (1%)
    dot_general x8, matrix products, apply_rows(): return jnp.einsum('kb,rbc->rkc', matrix, values_in, precision=exact_mode)  79.6 us
    reduce_scatter x1, waiting for transfers between devices, local(): lax.psum_scatter(partial_out, 'ch', scatter_dimension=1, tiled=True)  77.4 us
    all_to_all x1, blocking collectives, local(): lax.all_to_all(turned, 'seq', split_axis=2, concat_axis=1, tiled=True)  58.6 us
    all_gather x1, waiting for transfers between devices, local(): features_all = lax.all_gather(tokens, 'ch', axis=1, tiled=True)  53.5 us
    all_to_all x1, waiting for transfers between devices, local(): lax.all_to_all(outer_part, 'seq', split_axis=1, concat_axis=2, tiled=True)  40.3 us
    all_to_all x1, blocking collectives, local(): lax.all_to_all(partial_conv, 'seq', split_axis=0, concat_axis=1, tiled=True)  21.5 us
    all_to_all x1, waiting for transfers between devices, local(): lax.all_to_all(stacked, 'seq', split_axis=1, concat_axis=0, tiled=True)  16.9 us
    dot_general x1, matrix products, local(): jnp.einsum('td,dgc->gtc', features_all, w_in, preferred_element_type=jnp....  11 us
  transfers between devices with their start and end apart: 4, of which 4 were waited for; matrix products, arithmetic and copies ran while one was open for 2% of the time, Pallas kernels for 0%

commit v1 on v0

v1 whole, which is shorter than its diff:
```python
import numpy as np

import jax
import jax.numpy as jnp
from jax import lax
from jax.sharding import PartitionSpec as P

bf16 = jnp.bfloat16
f32 = jnp.float32


def tables(blocks, tok, chans):
    total = 2 * blocks * tok
    freq = np.arange(blocks + 1)
    outer = 2 * np.pi * (freq[:, None] * np.arange(blocks)[None, :] % (2 * blocks)) / (2 * blocks)
    eye = np.eye(chans)
    first = np.concatenate([np.kron(np.cos(outer), eye), np.kron(-np.sin(outer), eye)])
    last = np.concatenate([np.kron(np.cos(outer.T), eye), np.kron(-np.sin(outer.T), eye)], axis=1)
    pos = np.arange(tok)
    inner = 2 * np.pi * (pos[:, None] * pos[None, :] % tok) / tok
    c, s = np.cos(inner), np.sin(inner)
    forward = np.block([[c, -s], [s, c]])
    inverse = np.block([[c, s], [-s, c]])
    twist = 2 * np.pi * (freq[:, None] * pos[None, :]) / total
    twist = np.stack([np.cos(twist), np.sin(twist)])[:, :, None, :]
    return (
        first.astype(bf16),
        (last / total).astype(bf16),
        forward.astype(bf16),
        inverse.astype(bf16),
        twist.astype(np.float32),
    )


def mm(a, b):
    return jnp.dot(a, b, preferred_element_type=f32)


def convolve(signal, filt, blocks, tok, chans):
    first, last, forward, inverse, twist = tables(blocks, tok, chans)
    rows = (blocks + 1) * chans
    shape = (blocks + 1, chans, tok)
    part = mm(first, signal.reshape(blocks * chans, tok))
    pr, pi = part[:rows].reshape(shape), part[rows:].reshape(shape)
    tc, ts = twist
    q = jnp.concatenate([pr * tc + pi * ts, pi * tc - pr * ts], axis=2)
    x = mm(q.astype(bf16).reshape(rows, 2 * tok), forward)
    xr, xi = x[:, :tok].reshape(shape), x[:, tok:].reshape(shape)
    hr, hi = filt
    z = jnp.concatenate([xr * hr - xi * hi, xr * hi + xi * hr], axis=2)
    u = mm(z.astype(bf16).reshape(rows, 2 * tok), inverse)
    ur, ui = u[:, :tok].reshape(shape), u[:, tok:].reshape(shape)
    v = jnp.concatenate([ur * tc - ui * ts, ur * ts + ui * tc], axis=0)
    return mm(last, v.astype(bf16).reshape(2 * rows, tok)).astype(bf16).reshape(blocks, chans, tok)


def local(tokens, w_in, w_out, spectra):
    blocks = lax.axis_size("seq")
    pos = lax.axis_index("seq")
    tok = tokens.shape[0]
    width = w_in.shape[2]
    chans = width // blocks
    turned = jnp.swapaxes(spectra.astype(bf16), 2, 3)
    own = 2 * pos + jnp.arange(2)
    turned = jnp.where((own > blocks)[None, :, None, None], turned[..., ::-1], turned)
    turned = lax.all_to_all(turned, "seq", split_axis=2, concat_axis=1, tiled=True).astype(f32)
    low = turned[:, : blocks + 1]
    high = turned[:, blocks + 1 :][:, ::-1]
    zero = jnp.zeros_like(low[0, :1])
    filt = jnp.stack(
        [
            low[0] + jnp.concatenate([zero, high[0], zero]),
            low[1] - jnp.concatenate([zero, high[1], zero]),
        ]
    )
    features = lax.all_gather(tokens, "ch", axis=1, tiled=True)
    projected = jnp.einsum("td,dgc->gtc", features, w_in, preferred_element_type=f32).astype(bf16)
    signal = (projected[1].astype(f32) * projected[2].astype(f32)).astype(bf16).T
    signal = lax.all_to_all(signal.reshape(blocks, chans, tok), "seq", split_axis=0, concat_axis=0, tiled=True)
    conv = convolve(signal, filt, blocks, tok, chans)
    conv = lax.all_to_all(conv, "seq", split_axis=0, concat_axis=0, tiled=True)
    conv = conv.reshape(width, tok).T
    gated = (projected[0].astype(f32) * conv.astype(f32)).astype(bf16)
    partial_out = jnp.dot(gated, w_out, preferred_element_type=f32).astype(bf16)
    return lax.psum_scatter(partial_out, "ch", scatter_dimension=1, tiled=True)


def solution(mesh):
    in_specs = (P("seq", "ch"), P(None, None, "ch"), P("ch", None), P(None, "seq", None, "ch"))
    return jax.shard_map(local, mesh=mesh, in_specs=in_specs, out_specs=P("seq", "ch"), check_vma=False)
```

time: 457 us -> 191 us (0.42)
  waiting for transfers between devices: 189 us -> 56.3 us
  matrix products: 108 us -> 22.5 us
  blocking collectives: 80.2 us -> 52.2 us
  local copies, waits for them, and re-layouts: 42.4 us -> 28.6 us
  starting transfers between devices: 13.2 us -> 4.82 us
  other arithmetic: 6.26 us -> 12 us
    dot_general x14 -> x8, matrix products: 108 us -> 22.5 us  [the longest x1 11 us: local(): jnp.einsum('td,dgc->gtc', features, w_in, preferred_element_type=f32)]
    all_gather x1, waiting for transfers between devices: 53.5 us -> 0.01 us  [local(): features = lax.all_gather(tokens, 'ch', axis=1, tiled=True)]
    all_to_all x2 -> x1, waiting for transfers between devices: 57.2 us -> 9.81 us  [local(): lax.all_to_all(signal.reshape(blocks, chans, tok), 'seq', split_axis=0, c...]
    reduce_scatter x1, waiting for transfers between devices: 77.4 us -> 45.7 us  [local(): return lax.psum_scatter(partial_out, 'ch', scatter_dimension=1, tiled=True)]
    all_to_all x1, blocking collectives: 58.6 us -> 36.8 us  [local(): lax.all_to_all(turned, 'seq', split_axis=2, concat_axis=1, tiled=True)]
    rev x0 -> x1, local copies, waits for them, and re-layouts: none -> 15.7 us  [local(): turned[..., ::-1]]
    another operation x2 -> x0, local copies, waits for them, and re-layouts: 11.7 us -> none  [the longest x1 7.32 us: local(): jnp.stack([back_real * twist_cos - back_imag * twist_sin, back_imag * twi...]
    slice x7 -> x3, local copies, waits for them, and re-layouts: 12.5 us -> 1.94 us  [the longest x1 1.58 us: local(): low[0] + jnp.concatenate([zero, high[0], zero])]
  transfers between devices with their start and end apart: 4 -> 3, of which waited for: 4 -> 2; matrix products, arithmetic and copies ran while one was open for 2% -> 18% of each run, Pallas kernels for 0% -> 0%
where the time goes in v1:
time: 191 us; the launch traced here: 190 us
  waiting for transfers between devices  56.3 us (29%)
  blocking collectives  52.2 us (27%)
  local copies, waits for them, and re-layouts  28.6 us (15%)
  matrix products  22.5 us (12%)
  between operations  13.6 us (7%)
  other arithmetic  12 us (6%)
  starting transfers between devices  4.82 us (3%)
    reduce_scatter x1, waiting for transfers between devices, local(): return lax.psum_scatter(partial_out, 'ch', scatter_dimension=1, tiled=True)  45.7 us
    all_to_all x1, blocking collectives, local(): lax.all_to_all(turned, 'seq', split_axis=2, concat_axis=1, tiled=True)  36.8 us
    rev x1, local copies, waits for them, and re-layouts, local(): turned[..., ::-1]  15.7 us
    all_to_all x1, blocking collectives, local(): conv = lax.all_to_all(conv, 'seq', split_axis=0, concat_axis=0, tiled=True)  15.3 us
    dot_general x1, matrix products, local(): jnp.einsum('td,dgc->gtc', features, w_in, preferred_element_type=f32)  11 us
    all_to_all x1, waiting for transfers between devices, local(): lax.all_to_all(signal.reshape(blocks, chans, tok), 'seq', split_axis=0, c...  9.81 us
    unnamed x21, local copies, waits for them, and re-layouts  9.46 us
    dot_general x6, matrix products, mm(): return jnp.dot(a, b, preferred_element_type=f32)  6.05 us
  transfers between devices with their start and end apart: 3, of which 2 were waited for; matrix products, arithmetic and copies ran while one was open for 18% of the time, Pallas kernels for 0%

profile of v1, /device:TPU:1, one launch (start us, length us, event | category | flops | bytes accessed | tf_op | source)
XLA Modules:
  0.0 190.0 jit_solution(7134721626052784640)
XLA Ops:
  7.3 3.8 %convert_element_type.98 = bf16[2,2,512,512]{3,2,1,0:T(8,128)(2,1)} convert(f32[2,2,512,512]{3,2,1,0:T(8,128)} %param.13) | non-fusion elementwise | flops 1048576 | bytes 6291456 | tf_op jit(solution)/shard_map/convert_element_type | solution.py:63
  11.1 4.9 %copy.23 = bf16[2,2,512,512]{2,1,0,3:T(2,128)(2,1)S(1)} copy(bf16[2,2,512,512]{3,2,1,0:T(8,128)(2,1)} %convert_element_type.98) | data formatting | bytes 4194304
  16.0 15.7 %rev.4 = bf16[2,2,512,512]{3,1,0,2:T(2,128)(2,1)} reverse(bf16[2,2,512,512]{3,1,0,2:T(2,128)(2,1)S(1)} %bitcast.85), dimensions={3} | reverse | bytes 4194304 | tf_op jit(solution)/shard_map/rev | solution.py:65
  31.8 3.8 %broadcast_select_fusion = bf16[2,2,512,512]{3,1,0,2:T(2,128)(2,1)S(1)} fusion(bf16[2,2,512,512]{3,1,0,2:T(2,128)(2,1)} %rev.4, pred[2]{0:T(512)(128)(4,1)S(1)} %add_compare_fusion, bf16[2,2,512,512]{2,1,0,3:T(2,128)(2,1)S(1)} %copy.23), kind=kLoop, calls=%fused_computation.4 | loop fusion | flops 1048576 | bytes 6291458 | tf_op jit(solution)/shard_map/jit(_where)/select_n | solution.py:65
  35.6 36.8 %all_to_all.19 = bf16[2,2,512,512]{3,1,0,2:T(2,128)(2,1)S(1)} all-to-all(bf16[2,2,512,512]{3,1,0,2:T(2,128)(2,1)S(1)} %broadcast_select_fusion), channel_id=1, replica_groups=mesh['seq'=32,'ch'=4] {'seq'}, dimensions={2} | all-to-all | bytes 4194304 | tf_op jit(solution)/shard_map/all_to_all | solution.py:66
  73.4 0.8 copy.21
  74.9 1.6 fusion.16
  76.5 11.0 %fusion.5 = bf16[3,512,512]{1,2,0:T(8,128)(2,1)S(1)} fusion(bf16[4096,3,512]{2,0,1:T(8,128)(2,1)} %param.11, bf16[512,4096]{1,0:T(8,128)(2,1)} %all-gather.2.cloned.1.call-done), kind=kOutput, calls=%fused_computation.16 | convolution fusion | flops 6443237376 | bytes 18350080 | tf_op jit(solution)/shard_map/td,dgc->gtc/dot_general | solution.py:77
  87.5 1.2 copy-done.2
  88.6 0.9 multiply_convert_fusion
  89.6 4.6 %all-to-all-start = ((bf16[32,16,512]{2,1,0:T(8,128)(2,1)}), bf16[32,16,512]{2,1,0:T(8,128)(2,1)}, u32[]{:S(2)}, u32[]{:S(2)}) async-start(bf16[32,16,512]{2,1,0:T(8,128)(2,1)} %bitcast.5), calls=%async_computation | async-start | bytes 1048576 | tf_op jit(solution)/shard_map/all_to_all | solution.py:79
  94.4 1.5 bitcast_add_fusion
  96.1 9.8 %all-to-all-done = bf16[32,16,512]{2,1,0:T(8,128)(2,1)} async-done(((bf16[32,16,512]{2,1,0:T(8,128)(2,1)}), bf16[32,16,512]{2,1,0:T(8,128)(2,1)}, u32[]{:S(2)}, u32[]{:S(2)}) %all-to-all-start) | async-done | bytes 524320 | tf_op jit(solution)/shard_map/all_to_all | solution.py:79
  105.9 2.1 %fusion.19 = f32[1056,512]{1,0:T(8,128)S(1)} fusion(bf16[1056,512]{1,0:T(8,128)(2,1)} %constant.24.clone, bf16[512,512]{1,0:T(8,128)(2,1)} %bitcast.6), kind=kOutput, calls=%fused_computation.41 | convolution fusion | flops 553648128 | bytes 3768320 | tf_op jit(solution)/shard_map/dot_general | solution.py:36
  108.5 0.8 copy-done.6
  109.3 0.7 fusion.20
  110.5 0.7 convolution_add_fusion.1
  111.7 0.8 fusion.14
  112.9 0.8 convolution_add_fusion
  114.5 1.2 copy-done.9
  115.7 0.8 convolution_convert_fusion.1
  116.5 15.3 %all_to_all.20 = bf16[32,16,512]{2,1,0:T(8,128)(2,1)S(1)} all-to-all(bf16[32,16,512]{2,1,0:T(8,128)(2,1)S(1)} %bitcast.93), channel_id=1, replica_groups=mesh['seq'=32,'ch'=4] {'seq'}, dimensions={0} | all-to-all | bytes 1048576 | tf_op jit(solution)/shard_map/all_to_all | solution.py:81
  131.9 5.5 %convolution_convert_fusion = bf16[512,4096]{1,0:T(8,128)(2,1)} fusion(bf16[512,4096]{1,0:T(8,128)(2,1)S(1)} %copy-done.1, bf16[512,512]{1,0:T(8,128)(2,1)S(1)} %bitcast.91, bf16[3,512,512]{1,2,0:T(8,128)(2,1)} %copy-done.2), kind=kOutput, calls=%fused_computation | convolution fusion | flops 2150629376 | bytes 9437184 | tf_op jit(solution)/shard_map/dot_general | solution.py:84
  137.4 45.7 %reduce-scatter.2.cloned.1.call-done = bf16[512,1024]{1,0:T(8,128)(2,1)} async-done(((bf16[512,4096]{1,0:T(8,128)(2,1)}), bf16[512,1024]{1,0:T(8,128)(2,1)}) %reduce-scatter.2.cloned.1.call-update) | async-done | bytes 1048592 | tf_op jit(solution)/shard_map/reduce_scatter | solution.py:85
  (34 shorter events, 5.3 us)
Async XLA Ops:
  6.5 70.0 %all-gather.2.cloned.1.call-start = ((), (), s32[]{:S(2)}) async-start(), calls=%async_computation.4 | async-start | bytes 5242880 | tf_op jit(solution)/shard_map/all_gather | solution.py:76
  87.5 1.2 copy-start.2
  89.6 16.3 %all-to-all-start = ((bf16[32,16,512]{2,1,0:T(8,128)(2,1)}), bf16[32,16,512]{2,1,0:T(8,128)(2,1)}, u32[]{:S(2)}, u32[]{:S(2)}) async-start(bf16[32,16,512]{2,1,0:T(8,128)(2,1)} %bitcast.5), calls=%async_computation | async-start | bytes 1048576 | tf_op jit(solution)/shard_map/all_to_all | solution.py:79
  94.2 89.0 %reduce-scatter.2.cloned.1.call-start = ((), (), s32[]{:S(2)}) async-start(), calls=%async_computation.5 | async-start | bytes 5242880 | tf_op jit(solution)/shard_map/reduce_scatter | solution.py:85
  94.4 1.6 copy-start
  105.9 2.1 %copy-start.7 = (f32[33,512]{1,0:T(8,128)S(1)}, f32[33,512]{1,0:T(8,128)}, u32[]{:S(2)}) copy-start(f32[33,512]{1,0:T(8,128)} %constant.31) | copy-start | bytes 202756
  105.9 2.1 %copy-start.8 = (f32[33,512]{1,0:T(8,128)S(1)}, f32[33,512]{1,0:T(8,128)}, u32[]{:S(2)}) copy-start(f32[33,512]{1,0:T(8,128)} %constant.32) | copy-start | bytes 202756
  108.0 1.2 copy-start.6
  109.3 1.2 copy-start.5
  110.5 1.2 copy-start.4
  111.7 1.2 copy-start.3
  114.4 1.3 copy-start.9
  115.7 16.2 %copy-start.1 = (bf16[512,4096]{1,0:T(8,128)(2,1)S(1)}, bf16[512,4096]{1,0:T(8,128)(2,1)}, u32[]{:S(2)}) copy-start(bf16[512,4096]{1,0:T(8,128)(2,1)} %param.12) | copy-start | bytes 12582916
Sparse Core Ops, SparseCore 0:
  9.0 51.6 all-gather.1
  137.6 45.5 reduce-scatter.1

commit v2 on v1

v2 whole, which is shorter than its diff:
```python
import functools

import numpy as np

import jax
import jax.numpy as jnp
from jax import lax
from jax.experimental import pallas as pl
from jax.experimental.pallas import tpu as pltpu
from jax.sharding import PartitionSpec as P

bf16 = jnp.bfloat16
f32 = jnp.float32
MESH = pl.DeviceIdType.MESH


def tables(blocks, tok, chans):
    total = 2 * blocks * tok
    freq = np.arange(blocks + 1)
    outer = 2 * np.pi * (freq[:, None] * np.arange(blocks)[None, :] % (2 * blocks)) / (2 * blocks)
    eye = np.eye(chans)
    first = np.concatenate([np.kron(np.cos(outer), eye), np.kron(-np.sin(outer), eye)])
    last = np.concatenate([np.kron(np.cos(outer.T), eye), np.kron(-np.sin(outer.T), eye)], axis=1)
    pos = np.arange(tok)
    inner = 2 * np.pi * (pos[:, None] * pos[None, :] % tok) / tok
    c, s = np.cos(inner), np.sin(inner)
    forward = np.block([[c, -s], [s, c]])
    inverse = np.block([[c, s], [-s, c]])
    twist = 2 * np.pi * (freq[:, None] * pos[None, :]) / total
    twist = np.stack([np.cos(twist), np.sin(twist)])[:, :, None, :]
    return (
        first.astype(bf16),
        (last / total).astype(bf16),
        forward.astype(bf16),
        inverse.astype(bf16),
        twist.astype(np.float32),
    )


def mm(a, b):
    return jnp.dot(a, b, preferred_element_type=f32)


def mm_t(a, b):
    return lax.dot_general(a, b, (((1,), (1,)), ((), ())), preferred_element_type=f32)


def unit(n, flipped=None):
    row = lax.broadcasted_iota(jnp.int32, (n, n), 0)
    col = lax.broadcasted_iota(jnp.int32, (n, n), 1)
    if flipped is not None:
        row = jnp.where(flipped, n - 1 - row, row)
    return jnp.where(row == col, 1.0, 0.0).astype(bf16)


def kernel(
    nz, blocks, tok, chans,
    tokens_hbm, w_in_hbm, w_out_hbm, spectra_hbm, first_hbm, last_hbm, forward_hbm, inverse_hbm, twist_hbm,
    out_ref,
    feat, w_in, w_out, spec, first, last, forward, inverse, twist,
    acc, hsend, hrecv, filt, sig, xrecv, part, q, v, y, conv, qt,
    opp_send, opp_recv, side, side_send, side_recv,
    load_sem, ag_send, ag_recv, h_send, h_recv, s_send, s_recv, c_send, c_recv, r_send, r_recv,
):
    me = lax.axis_index("seq")
    z = lax.axis_index("ch")
    right, left, opp = lax.rem(z + 1, nz), lax.rem(z + nz - 1, nz), lax.rem(z + 2, nz)
    width = chans * blocks
    depth = tokens_hbm.shape[1]
    half = tok // 2
    top, low = pl.ds(0, half), pl.ds(half, half)
    rows = (blocks + 1) * chans

    def load(src, dst, sem):
        return pltpu.make_async_copy(src, dst, load_sem.at[sem])

    def load_w(block, sem):
        at = pl.ds(pl.multiple_of(block * depth, depth), depth)
        return load(w_in_hbm.at[:, at], w_in.at[:, at], sem)

    tok_load = load(tokens_hbm, feat.at[z], 0)
    spec_load = load(spectra_hbm, spec, 1)
    w_loads = [load_w(z, 2), load_w(left, 3), load_w(right, 4), load_w(opp, 5)]
    rest = [
        load(w_out_hbm, w_out, 6), load(first_hbm, first, 7), load(last_hbm, last, 8),
        load(forward_hbm, forward, 9), load(inverse_hbm, inverse, 10), load(twist_hbm, twist, 11),
    ]
    tok_load.start()
    spec_load.start()
    for copy in w_loads + rest:
        copy.start()

    barrier = pltpu.get_barrier_semaphore()
    for near in (left, right):
        pl.semaphore_signal(barrier, inc=1, device_id=(me, near), device_id_type=MESH)

    @pl.loop(1, blocks)
    def _(k):
        pl.semaphore_signal(barrier, inc=1, device_id=(lax.rem(me + k, blocks), z), device_id_type=MESH)

    pl.semaphore_wait(barrier, blocks + 1)
    tok_load.wait()

    def hop(block, at, sem, to):
        return pltpu.make_async_remote_copy(
            src_ref=feat.at[block, at], dst_ref=feat.at[block, at],
            send_sem=ag_send.at[sem], recv_sem=ag_recv.at[sem],
            device_id=(me, to), device_id_type=MESH,
        )

    gather = [hop(z, top, 0, right), hop(z, low, 1, left), hop(z, low, 2, right), hop(z, top, 3, left)]
    for copy in gather:
        copy.start()

    def swap(src, dst, send, recv, peer, entry):
        return pltpu.make_async_remote_copy(
            src_ref=src.at[peer], dst_ref=dst.at[entry],
            send_sem=send.at[peer], recv_sem=recv.at[entry],
            device_id=(peer, z), device_id_type=MESH,
        )

    def swap_start(*refs):
        @pl.loop(1, blocks)
        def _(k):
            swap(*refs, lax.rem(me + k, blocks), me).start()

    def swap_arrived(*refs):
        @pl.loop(1, blocks)
        def _(k):
            peer = lax.rem(me + k, blocks)
            swap(*refs, peer, peer).wait_recv()

    def swap_sent(*refs):
        @pl.loop(1, blocks)
        def _(k):
            swap(*refs, lax.rem(me + k, blocks), me).wait_send()

    h_refs = (hsend, hrecv, h_send, h_recv)
    spec_load.wait()
    for a in range(2):
        for ri in range(2):
            turned = mm_t(unit(width), spec[ri, a].astype(bf16)).astype(bf16)
            turned = mm(turned, unit(tok, 2 * me + a > blocks)).astype(bf16)
            hsend[:, ri, a] = turned.reshape(blocks, chans, tok)
    swap_start(*h_refs)
    hrecv[pl.ds(me, 1)] = hsend[pl.ds(me, 1)]

    def project(block, start, count, fresh=False):
        at = pl.ds(pl.multiple_of(block * depth, depth), depth)

        @pl.loop(0, 3)
        def _(g):
            for r in range(start, start + count, half):
                term = mm(feat[block, r:r + half], w_in[g, at])
                if fresh:
                    acc[g, r:r + half] = term
                else:
                    acc[g, r:r + half] += term

    w_loads[0].wait()
    project(z, 0, tok, True)
    hop(left, top, 0, right).wait_recv()
    far_top = hop(left, top, 4, right)
    far_top.start()
    hop(right, low, 1, left).wait_recv()
    far_low = hop(right, low, 5, left)
    far_low.start()
    w_loads[1].wait()
    w_loads[2].wait()
    project(left, 0, half)
    project(right, half, half)
    hop(left, low, 2, right).wait_recv()
    project(left, half, half)
    hop(right, top, 3, left).wait_recv()
    project(right, 0, half)
    w_loads[3].wait()
    hop(opp, top, 4, right).wait_recv()
    project(opp, 0, half)
    hop(opp, low, 5, left).wait_recv()
    project(opp, half, half)

    s_refs = (sig, xrecv, s_send, s_recv)
    signal = (acc[1].astype(bf16).astype(f32) * acc[2].astype(bf16).astype(f32)).astype(bf16)
    sig[...] = mm_t(unit(width), signal).astype(bf16).reshape(blocks, chans, tok)
    swap_start(*s_refs)
    xrecv[pl.ds(me, 1)] = sig[pl.ds(me, 1)]
    qt[...] = mm_t(unit(width), acc[0].astype(bf16)).astype(bf16)

    swap_arrived(*h_refs)
    filt[:, 0] = hrecv[0, :, 0].astype(f32)
    filt[:, blocks] = hrecv[blocks // 2, :, 0].astype(f32)

    @pl.loop(1, blocks)
    def _(a):
        other = 2 * blocks - a
        near = hrecv[a // 2, :, a % 2].astype(f32)
        far = hrecv[other // 2, :, other % 2].astype(f32)
        filt[0, a] = near[0] + far[0]
        filt[1, a] = near[1] - far[1]

    for copy in rest:
        copy.wait()
    swap_arrived(*s_refs)

    x = xrecv[...].reshape(blocks * chans, tok)
    for i in range(2):
        part[i] = mm(first[i * rows:(i + 1) * rows], x)

    def at(a):
        return pl.ds(pl.multiple_of(a * chans, chans), chans)

    @pl.loop(0, blocks + 1)
    def _(a):
        pr, pi = part[0, at(a)], part[1, at(a)]
        tc, ts = twist[0, a], twist[1, a]
        q[at(a), :tok] = (pr * tc + pi * ts).astype(bf16)
        q[at(a), tok:] = (pi * tc - pr * ts).astype(bf16)

    def inner(table):
        for i in range(2):
            part[i] = mm(q[...], table[:, i * tok:(i + 1) * tok])

    inner(forward)

    @pl.loop(0, blocks + 1)
    def _(a):
        xr, xi = part[0, at(a)], part[1, at(a)]
        hr, hi = filt[0, a], filt[1, a]
        q[at(a), :tok] = (xr * hr - xi * hi).astype(bf16)
        q[at(a), tok:] = (xr * hi + xi * hr).astype(bf16)

    inner(inverse)

    @pl.loop(0, blocks + 1)
    def _(a):
        ur, ui = part[0, at(a)], part[1, at(a)]
        tc, ts = twist[0, a], twist[1, a]
        v[0, at(a)] = (ur * tc - ui * ts).astype(bf16)
        v[1, at(a)] = (ur * ts + ui * tc).astype(bf16)

    c_refs = (y, conv, c_send, c_recv)
    y[...] = mm(last[...], v[...].reshape(2 * rows, tok)).astype(bf16).reshape(blocks, chans, tok)
    swap_start(*c_refs)
    conv[pl.ds(me, 1)] = y[pl.ds(me, 1)]
    swap_arrived(*c_refs)

    gated_t = (qt[...].astype(f32) * conv[...].reshape(width, tok).astype(f32)).astype(bf16)
    gated = mm_t(unit(tok), gated_t).astype(bf16)

    def term(block, start):
        cols = pl.ds(pl.multiple_of(block * depth, depth), depth)
        return mm(gated[start:start + half], w_out[:, cols])

    def give(src, dst, sem, to):
        return pltpu.make_async_remote_copy(
            src_ref=src, dst_ref=dst, send_sem=r_send.at[sem], recv_sem=r_recv.at[sem],
            device_id=(me, to), device_id_type=MESH,
        )

    def opp_give(i, to):
        return give(opp_send.at[i], opp_recv.at[i], i, to)

    def side_give(i, h, to):
        return give(side_send.at[i, h], side_recv.at[i, h], 2 + 2 * i + h, to)

    gives = [
        opp_give(0, right), opp_give(1, left), side_give(0, 1, right), side_give(1, 0, left),
        side_give(0, 0, right), side_give(1, 1, left),
    ]
    opp_send[0] = term(opp, 0).astype(bf16)
    gives[0].start()
    opp_send[1] = term(opp, half).astype(bf16)
    gives[1].start()
    side_send[0, 1] = term(right, half).astype(bf16)
    gives[2].start()
    side_send[1, 0] = term(left, 0).astype(bf16)
    gives[3].start()
    side[0] = term(right, 0)
    side[1] = term(left, half)
    opp_give(0, right).wait_recv()
    side_send[0, 0] = (side[0] + opp_recv[0].astype(f32)).astype(bf16)
    gives[4].start()
    opp_give(1, left).wait_recv()
    side_send[1, 1] = (side[1] + opp_recv[1].astype(f32)).astype(bf16)
    gives[5].start()
    side[0] = term(z, 0)
    side[1] = term(z, half)
    side_give(0, 1, right).wait_recv()
    side_give(1, 0, left).wait_recv()
    side[1] += side_recv[0, 1].astype(f32)
    side[0] += side_recv[1, 0].astype(f32)
    side_give(0, 0, right).wait_recv()
    out_ref[:half] = (side[0] + side_recv[0, 0].astype(f32)).astype(bf16)
    side_give(1, 1, left).wait_recv()
    out_ref[half:] = (side[1] + side_recv[1, 1].astype(f32)).astype(bf16)

    for copy in gather + [far_top, far_low] + gives:
        copy.wait_send()
    swap_sent(*h_refs)
    swap_sent(*s_refs)
    swap_sent(*c_refs)


def local(nz, blocks, tokens, w_in, w_out, spectra):
    tok, depth = tokens.shape
    width = w_in.shape[2]
    chans = width // blocks
    rows = (blocks + 1) * chans
    half = tok // 2
    consts = [jnp.asarray(t) for t in tables(blocks, tok, chans)]
    dma = pltpu.SemaphoreType.DMA
    vmem = pltpu.VMEM
    scratch = [
        vmem((nz, tok, depth), bf16),
        vmem((3, nz * depth, width), bf16),
        vmem(w_out.shape, bf16),
        vmem(spectra.shape, f32),
        *[vmem(t.shape, t.dtype) for t in consts],
        vmem((3, tok, width), f32),
        vmem((blocks, 2, 2, chans, tok), bf16),
        vmem((blocks, 2, 2, chans, tok), bf16),
        vmem((2, blocks + 1, chans, tok), f32),
        vmem((blocks, chans, tok), bf16),
        vmem((blocks, chans, tok), bf16),
        vmem((2, rows, tok), f32),
        vmem((rows, 2 * tok), bf16),
        vmem((2, rows, tok), bf16),
        vmem((blocks, chans, tok), bf16),
        vmem((blocks, chans, tok), bf16),
        vmem((width, tok), bf16),
        vmem((2, half, depth), bf16),
        vmem((2, half, depth), bf16),
        vmem((2, half, depth), f32),
        vmem((2, 2, half, depth), bf16),
        vmem((2, 2, half, depth), bf16),
        dma((12,)),
        dma((6,)), dma((6,)),
        dma((blocks,)), dma((blocks,)),
        dma((blocks,)), dma((blocks,)),
        dma((blocks,)), dma((blocks,)),
        dma((6,)), dma((6,)),
    ]
    return pl.pallas_call(
        functools.partial(kernel, nz, blocks, tok, chans),
        out_shape=jax.ShapeDtypeStruct((tok, depth), bf16),
        in_specs=[pl.BlockSpec(memory_space=pl.ANY)] * 9,
        out_specs=pl.BlockSpec(memory_space=pltpu.VMEM),
        scratch_shapes=scratch,
        compiler_params=pltpu.CompilerParams(
            collective_id=0, has_side_effects=True, vmem_limit_bytes=62 * 1024 * 1024
        ),
    )(tokens, jnp.swapaxes(w_in, 0, 1), w_out, spectra, *consts)


def solution(mesh):
    in_specs = (P("seq", "ch"), P(None, None, "ch"), P("ch", None), P(None, "seq", None, "ch"))
    body = functools.partial(local, mesh.shape["ch"], mesh.shape["seq"])
    return jax.shard_map(body, mesh=mesh, in_specs=in_specs, out_specs=P("seq", "ch"), check_vma=False)
```

time: 191 us -> 113 us (0.59)
  Pallas kernels: 0 us -> 110 us
  waiting for transfers between devices: 56.3 us -> 0 us
  blocking collectives: 52.2 us -> 0 us
  local copies, waits for them, and re-layouts: 28.6 us -> 2.26 us
  matrix products: 22.5 us -> 0 us
  between operations: 13.6 us -> 0.01 us
  other arithmetic: 12 us -> 0 us
  starting transfers between devices: 4.82 us -> 0 us
    pallas_call x0 -> x1, Pallas kernels: none -> 110 us  [local(): pl.pallas_call(functools.partial(kernel, nz, blocks, tok, chans), out_sha...]
    all_to_all x2 -> x0, blocking collectives: 52.2 us -> none  [the longest x1 36.8 us: local(): lax.all_to_all(turned, 'seq', split_axis=2, concat_axis=1, tiled=True)]
    reduce_scatter x1 -> x0, waiting for transfers between devices: 45.7 us -> none  [local(): return lax.psum_scatter(partial_out, 'ch', scatter_dimension=1, tiled=True)]
    dot_general x8 -> x0, matrix products: 22.5 us -> none  [the longest x1 11 us: local(): jnp.einsum('td,dgc->gtc', features, w_in, preferred_element_type=f32)]
    rev x1 -> x0, local copies, waits for them, and re-layouts: 15.7 us -> none  [local(): turned[..., ::-1]]
    all_to_all x1 -> x0, waiting for transfers between devices: 9.81 us -> none  [local(): lax.all_to_all(signal.reshape(blocks, chans, tok), 'seq', split_axis=0, c...]
    unnamed x21 -> x1, local copies, waits for them, and re-layouts: 9.46 us -> 2.26 us
    convert_element_type x3 -> x0, other arithmetic: 5.28 us -> none  [the longest x1 3.8 us: local(): turned = jnp.swapaxes(spectra.astype(bf16), 2, 3)]
  transfers between devices with their start and end apart: 3 -> 0, of which waited for: 2 -> 0; matrix products, arithmetic and copies ran while one was open for 18% -> 0% of each run, Pallas kernels for 0% -> 0%
where the time goes in v2:
time: 113 us
  Pallas kernels  110 us (97%)
  local copies, waits for them, and re-layouts  2.26 us (2%)
    pallas_call x1, Pallas kernels, local(): pl.pallas_call(functools.partial(kernel, nz, blocks, tok, chans), out_sha...  110 us
    unnamed x1, local copies, waits for them, and re-layouts  2.26 us

profile of v2, /device:TPU:1, one launch (start us, length us, event | category | flops | bytes accessed | tf_op | source)
XLA Modules:
  0.0 112.7 jit_solution(14009260707162536169)
XLA Ops:
  0.0 110.4 %shard_map.91 = bf16[512,1024]{1,0:T(8,128)(2,1)} custom-call(bf16[512,1024]{1,0:T(8,128)(2,1)} %tokens_hbm.1, bf16[3,4096,512]{2,1,0:T(8,128)(2,1)} %bitcast.1, bf16[512,4096]{1,0:T(8,128)(2,1)} %w_out_hbm.1, f32[2,2,512,512]{3,2,1,0:T(8,128)} %spectra_hbm.1, bf16[1056,512]{1,0:T(8,128)(2,1)} %constant.10.clone.first_hbm, ...), custom_call_target="tpu_custom_call" | custom-call | tf_op jit(solution)/shard_map/pallas_call | solution.py:343
  110.4 2.3 %copy.11 = bf16[512,1024]{1,0:T(8,128)(2,1)} copy(bf16[512,1024]{1,0:T(8,128)(2,1)} %shard_map.91) | data formatting | bytes 2097152

commit v3 on v2

--- a/solution.py
+++ b/solution.py
@@ -57,10 +57,10 @@
     nz, blocks, tok, chans,
     tokens_hbm, w_in_hbm, w_out_hbm, spectra_hbm, first_hbm, last_hbm, forward_hbm, inverse_hbm, twist_hbm,
     out_ref,
-    feat, w_in, w_out, spec, first, last, forward, inverse, twist,
+    feat, w_in, w_cols, w_relay, spec, first, last, forward, inverse, twist,
     acc, hsend, hrecv, filt, sig, xrecv, part, q, v, y, conv, qt,
-    opp_send, opp_recv, side, side_send, side_recv,
-    load_sem, ag_send, ag_recv, h_send, h_recv, s_send, s_recv, c_send, c_recv, r_send, r_recv,
+    gall, side,
+    load_sem, ag_send, ag_recv, h_send, h_recv, s_send, s_recv, c_send, c_recv, r_send, r_recv, w_send, w_recv,
 ):
     me = lax.axis_index("seq")
     z = lax.axis_index("ch")
@@ -82,7 +82,7 @@
     spec_load = load(spectra_hbm, spec, 1)
     w_loads = [load_w(z, 2), load_w(left, 3), load_w(right, 4), load_w(opp, 5)]
     rest = [
-        load(w_out_hbm, w_out, 6), load(first_hbm, first, 7), load(last_hbm, last, 8),
+        load(first_hbm, first, 7), load(last_hbm, last, 8),
         load(forward_hbm, forward, 9), load(inverse_hbm, inverse, 10), load(twist_hbm, twist, 11),
     ]
     tok_load.start()
@@ -100,6 +100,51 @@
 
     pl.semaphore_wait(barrier, blocks + 1)
     tok_load.wait()
+
+    core = lax.rem(me, 2)
+    sibling = me + 1 - 2 * core
+    part_w = width // 2
+
+    def w_rows(c, start=0, count=part_w):
+        return pl.ds(pl.multiple_of(c * part_w, part_w) + start, count)
+
+    def w_give(src, dst, sem, to, line=me):
+        return pltpu.make_async_remote_copy(
+            src_ref=src, dst_ref=dst, send_sem=w_send.at[sem], recv_sem=w_recv.at[sem],
+            device_id=(line, to), device_id_type=MESH,
+        )
+
+    def w_slice(rows_at, block):
+        return w_out_hbm.at[rows_at, pl.ds(pl.multiple_of(block * depth, depth), depth)]
+
+    quarter = part_w // 2
+    first_q, second_q = w_rows(core, 0, quarter), w_rows(core, quarter, quarter)
+    w_near = [
+        w_give(w_slice(first_q, opp), w_relay.at[0], 2, right),
+        w_give(w_slice(second_q, opp), w_relay.at[1], 3, left),
+        w_give(w_slice(w_rows(core), right), w_cols.at[z, w_rows(core)], 0, right),
+        w_give(w_slice(w_rows(core), left), w_cols.at[z, w_rows(core)], 1, left),
+    ]
+    w_got = [
+        w_give(w_relay.at[0], w_relay.at[0], 2, right),
+        w_give(w_relay.at[1], w_relay.at[1], 3, left),
+        w_give(w_cols.at[left, w_rows(core)], w_cols.at[left, w_rows(core)], 0, right),
+        w_give(w_cols.at[right, w_rows(core)], w_cols.at[right, w_rows(core)], 1, left),
+    ]
+    w_fwd = [
+        w_give(w_relay.at[0], w_cols.at[left, first_q], 4, right),
+        w_give(w_relay.at[1], w_cols.at[right, second_q], 5, left),
+    ]
+
+    def w_shares(c):
+        return [
+            w_give(w_cols.at[block, w_rows(c)], w_cols.at[block, w_rows(c)], 6 + i, z, sibling)
+            for i, block in enumerate((left, right, opp))
+        ]
+
+    w_share, w_theirs = w_shares(core), w_shares(1 - core)
+    own_w = load(w_slice(pl.ds(0, width), z), w_cols.at[z], 6)
+    own_w.start()
 
     def hop(block, at, sem, to):
         return pltpu.make_async_remote_copy(
@@ -177,6 +222,8 @@
     hop(opp, top, 4, right).wait_recv()
     project(opp, 0, half)
     hop(opp, low, 5, left).wait_recv()
+    for copy in w_near:
+        copy.start()
     project(opp, half, half)
 
     s_refs = (sig, xrecv, s_send, s_recv)
@@ -202,6 +249,11 @@
         copy.wait()
     swap_arrived(*s_refs)
 
+    w_got[0].wait_recv()
+    w_fwd[0].start()
+    w_got[1].wait_recv()
+    w_fwd[1].start()
+
     x = xrecv[...].reshape(blocks * chans, tok)
     for i in range(2):
         part[i] = mm(first[i * rows:(i + 1) * rows], x)
@@ -242,58 +294,56 @@
     y[...] = mm(last[...], v[...].reshape(2 * rows, tok)).astype(bf16).reshape(blocks, chans, tok)
     swap_start(*c_refs)
     conv[pl.ds(me, 1)] = y[pl.ds(me, 1)]
+    w_got[2].wait_recv()
+    w_share[0].start()
+    w_got[3].wait_recv()
+    w_share[1].start()
     swap_arrived(*c_refs)
 
     gated_t = (qt[...].astype(f32) * conv[...].reshape(width, tok).astype(f32)).astype(bf16)
-    gated = mm_t(unit(tok), gated_t).astype(bf16)
-
-    def term(block, start):
-        cols = pl.ds(pl.multiple_of(block * depth, depth), depth)
-        return mm(gated[start:start + half], w_out[:, cols])
-
-    def give(src, dst, sem, to):
+    gall[pl.ds(z, 1)] = mm_t(unit(tok), gated_t).astype(bf16)[None]
+
+    def ghop(block, at, sem, to):
         return pltpu.make_async_remote_copy(
-            src_ref=src, dst_ref=dst, send_sem=r_send.at[sem], recv_sem=r_recv.at[sem],
+            src_ref=gall.at[block, at], dst_ref=gall.at[block, at],
+            send_sem=r_send.at[sem], recv_sem=r_recv.at[sem],
             device_id=(me, to), device_id_type=MESH,
         )
 
-    def opp_give(i, to):
-        return give(opp_send.at[i], opp_recv.at[i], i, to)
-
-    def side_give(i, h, to):
-        return give(side_send.at[i, h], side_recv.at[i, h], 2 + 2 * i + h, to)
-
-    gives = [
-        opp_give(0, right), opp_give(1, left), side_give(0, 1, right), side_give(1, 0, left),
-        side_give(0, 0, right), side_give(1, 1, left),
-    ]
-    opp_send[0] = term(opp, 0).astype(bf16)
-    gives[0].start()
-    opp_send[1] = term(opp, half).astype(bf16)
-    gives[1].start()
-    side_send[0, 1] = term(right, half).astype(bf16)
-    gives[2].start()
-    side_send[1, 0] = term(left, 0).astype(bf16)
-    gives[3].start()
-    side[0] = term(right, 0)
-    side[1] = term(left, half)
-    opp_give(0, right).wait_recv()
-    side_send[0, 0] = (side[0] + opp_recv[0].astype(f32)).astype(bf16)
-    gives[4].start()
-    opp_give(1, left).wait_recv()
-    side_send[1, 1] = (side[1] + opp_recv[1].astype(f32)).astype(bf16)
-    gives[5].start()
+    gives = [ghop(z, top, 0, right), ghop(z, low, 1, left), ghop(z, low, 2, right), ghop(z, top, 3, left)]
+    for copy in gives:
+        copy.start()
+
+    def term(block, h):
+        return mm(gall[block, h * half:(h + 1) * half], w_cols[block])
+
+    w_fwd[0].wait_recv()
+    w_fwd[1].wait_recv()
+    w_share[2].start()
+    own_w.wait()
     side[0] = term(z, 0)
-    side[1] = term(z, half)
-    side_give(0, 1, right).wait_recv()
-    side_give(1, 0, left).wait_recv()
-    side[1] += side_recv[0, 1].astype(f32)
-    side[0] += side_recv[1, 0].astype(f32)
-    side_give(0, 0, right).wait_recv()
-    out_ref[:half] = (side[0] + side_recv[0, 0].astype(f32)).astype(bf16)
-    side_give(1, 1, left).wait_recv()
-    out_ref[half:] = (side[1] + side_recv[1, 1].astype(f32)).astype(bf16)
-
+    side[1] = term(z, 1)
+    ghop(left, top, 0, right).wait_recv()
+    far_gtop = ghop(left, top, 4, right)
+    far_gtop.start()
+    ghop(right, low, 1, left).wait_recv()
+    far_glow = ghop(right, low, 5, left)
+    far_glow.start()
+    w_theirs[0].wait_recv()
+    w_theirs[1].wait_recv()
+    side[0] += term(left, 0)
+    side[1] += term(right, 1)
+    ghop(left, low, 2, right).wait_recv()
+    side[1] += term(left, 1)
+    ghop(right, top, 3, left).wait_recv()
+    side[0] += term(right, 0)
+    w_theirs[2].wait_recv()
+    ghop(opp, top, 4, right).wait_recv()
+    out_ref[:half] = (side[0] + term(opp, 0)).astype(bf16)
+    ghop(opp, low, 5, left).wait_recv()
+    out_ref[half:] = (side[1] + term(opp, 1)).astype(bf16)
+
+    gives += [far_gtop, far_glow] + w_near + w_fwd + w_share
     for copy in gather + [far_top, far_low] + gives:
         copy.wait_send()
     swap_sent(*h_refs)
@@ -313,7 +363,8 @@
     scratch = [
         vmem((nz, tok, depth), bf16),
         vmem((3, nz * depth, width), bf16),
-        vmem(w_out.shape, bf16),
+        vmem((nz, width, depth), bf16),
+        vmem((2, width // 4, depth), bf16),
         vmem(spectra.shape, f32),
         *[vmem(t.shape, t.dtype) for t in consts],
         vmem((3, tok, width), f32),
@@ -328,17 +379,15 @@
         vmem((blocks, chans, tok), bf16),
         vmem((blocks, chans, tok), bf16),
         vmem((width, tok), bf16),
-        vmem((2, half, depth), bf16),
-        vmem((2, half, depth), bf16),
+        vmem((nz, tok, width), bf16),
         vmem((2, half, depth), f32),
-        vmem((2, 2, half, depth), bf16),
-        vmem((2, 2, half, depth), bf16),
         dma((12,)),
         dma((6,)), dma((6,)),
         dma((blocks,)), dma((blocks,)),
         dma((blocks,)), dma((blocks,)),
         dma((blocks,)), dma((blocks,)),
         dma((6,)), dma((6,)),
+        dma((9,)), dma((9,)),
     ]
     return pl.pallas_call(
         functools.partial(kernel, nz, blocks, tok, chans),

time: 113 us -> 96.9 us (0.86)
  Pallas kernels: 110 us -> 94.5 us
    pallas_call x1, Pallas kernels: 110 us -> 94.5 us  [local(): pl.pallas_call(functools.partial(kernel, nz, blocks, tok, chans), out_sha...]
where the time goes in v3:
time: 96.9 us; the launch traced here: 96.8 us
  Pallas kernels  94.5 us (98%)
  local copies, waits for them, and re-layouts  2.26 us (2%)
    pallas_call x1, Pallas kernels, local(): pl.pallas_call(functools.partial(kernel, nz, blocks, tok, chans), out_sha...  94.5 us
    unnamed x1, local copies, waits for them, and re-layouts  2.26 us

profile of v3, /device:TPU:1, one launch (start us, length us, event | category | flops | bytes accessed | tf_op | source)
XLA Modules:
  0.0 96.8 jit_solution(917806620728323301)
XLA Ops:
  0.0 94.5 %shard_map.91 = bf16[512,1024]{1,0:T(8,128)(2,1)} custom-call(bf16[512,1024]{1,0:T(8,128)(2,1)} %tokens_hbm.1, bf16[3,4096,512]{2,1,0:T(8,128)(2,1)} %bitcast.1, bf16[512,4096]{1,0:T(8,128)(2,1)} %w_out_hbm.1, f32[2,2,512,512]{3,2,1,0:T(8,128)} %spectra_hbm.1, bf16[1056,512]{1,0:T(8,128)(2,1)} %constant.10.clone.first_hbm, ...), custom_call_target="tpu_custom_call" | custom-call | tf_op jit(solution)/shard_map/pallas_call | solution.py:392
  94.5 2.3 %copy.11 = bf16[512,1024]{1,0:T(8,128)(2,1)} copy(bf16[512,1024]{1,0:T(8,128)(2,1)} %shard_map.91) | data formatting | bytes 2097152

commit v4 on v3

v4 whole, which is shorter than its diff:
```python
import functools

import numpy as np

import jax
import jax.numpy as jnp
from jax import lax
from jax.experimental import pallas as pl
from jax.experimental.pallas import tpu as pltpu
from jax.sharding import PartitionSpec as P

bf16 = jnp.bfloat16
f32 = jnp.float32
MESH = pl.DeviceIdType.MESH
IN_PARTS = (2, 2)
OUT_PARTS = (1, 1, 2)


def spans(parts, tok):
    ends = np.cumsum((0,) + parts) * (tok // sum(parts))
    return [(int(a), int(b - a)) for a, b in zip(ends[:-1], ends[1:])]


def tables(blocks, tok, chans, chunks, outs):
    total = 2 * blocks * tok
    freq = np.arange(blocks + 1)
    outer = 2 * np.pi * (freq[:, None] * np.arange(blocks)[None, :] % (2 * blocks)) / (2 * blocks)
    eye = np.eye(chans)
    first = np.concatenate([np.kron(np.cos(outer), eye), np.kron(-np.sin(outer), eye)])
    last = np.concatenate([np.kron(np.cos(outer.T), eye), np.kron(-np.sin(outer.T), eye)], axis=1)
    pos = np.arange(tok)
    inner = 2 * np.pi * (pos[:, None] * pos[None, :] % tok) / tok
    c, s = np.cos(inner), np.sin(inner)
    def order(parts):
        return np.concatenate([np.arange(a, a + n) + i * tok for a, n in parts for i in range(2)])

    forward = np.block([[c, -s], [s, c]])[order(chunks)]
    inverse = np.block([[c, s], [-s, c]])[:, order(outs)]
    twist = 2 * np.pi * (freq[:, None] * pos[None, :]) / total
    twist = np.stack([np.cos(twist), np.sin(twist)])[:, :, None, :]
    return (
        first.astype(bf16),
        (last / total).astype(bf16),
        forward.astype(bf16),
        inverse.astype(bf16),
        twist.astype(np.float32),
    )


def mm(a, b):
    return jnp.dot(a, b, preferred_element_type=f32)


def mm_t(a, b):
    return lax.dot_general(a, b, (((1,), (1,)), ((), ())), preferred_element_type=f32)


def unit(n, flipped=None):
    row = lax.broadcasted_iota(jnp.int32, (n, n), 0)
    col = lax.broadcasted_iota(jnp.int32, (n, n), 1)
    if flipped is not None:
        row = jnp.where(flipped, n - 1 - row, row)
    return jnp.where(row == col, 1.0, 0.0).astype(bf16)


def kernel(
    nz, blocks, tok, chans, chunks, outs,
    tokens_hbm, w_in_hbm, w_out_hbm, spectra_hbm, first_hbm, last_hbm, forward_hbm, inverse_hbm, twist_hbm,
    out_hbm,
    feat, w_in, w_cols, w_relay, spec, first, last, forward, inverse, twist,
    acc, hsend, hrecv, filt, sig, xrecv, tmp, part, q, back, v, y, conv, qt,
    gall, side, stage,
    load_sem, ag_send, ag_recv, x_send, x_recv, r_send, r_recv, w_send, w_recv,
):
    me = lax.axis_index("seq")
    z = lax.axis_index("ch")
    right, left, opp = lax.rem(z + 1, nz), lax.rem(z + nz - 1, nz), lax.rem(z + 2, nz)
    width = chans * blocks
    depth = tokens_hbm.shape[1]

    def load(src, dst, sem):
        return pltpu.make_async_copy(src, dst, load_sem.at[sem])

    def load_w(block, sem):
        at = pl.ds(pl.multiple_of(block * depth, depth), depth)
        return load(w_in_hbm.at[:, at], w_in.at[:, at], sem)

    tok_load = load(tokens_hbm, feat.at[z], 0)
    spec_load = load(spectra_hbm, spec, 1)
    w_loads = [load_w(z, 2), load_w(left, 3), load_w(right, 4), load_w(opp, 5)]
    rest = [
        load(first_hbm, first, 7), load(last_hbm, last, 8),
        load(forward_hbm, forward, 9), load(inverse_hbm, inverse, 10), load(twist_hbm, twist, 11),
    ]
    tok_load.start()
    spec_load.start()
    for copy in w_loads + rest:
        copy.start()

    barrier = pltpu.get_barrier_semaphore()
    for near in (left, right):
        pl.semaphore_signal(barrier, inc=1, device_id=(me, near), device_id_type=MESH)

    def peers(act):
        mid = blocks // 2
        for low, high in ((mid, blocks), (blocks + 1, blocks + mid)):
            @pl.loop(low, high, unroll=True)
            def _(k):
                act(lax.rem(me + k, blocks))

    peers(lambda peer: pl.semaphore_signal(barrier, inc=1, device_id=(peer, z), device_id_type=MESH))
    pl.semaphore_wait(barrier, blocks + 1)
    tok_load.wait()

    core = lax.rem(me, 2)
    sibling = me + 1 - 2 * core
    line = 4 if blocks >= 32 else blocks // 2
    at_x, at_y = lax.rem(me // 2, line), me // (2 * line)
    even_x = 1 - lax.rem(at_x, 2)
    pair_x = me + 4 * even_x - 2
    if blocks >= 32:
        even_y = 1 - lax.rem(at_y, 2)
        pair_y = me + 2 * line * (2 * even_y - 1)
        pair_far = me + 2 * (lax.rem(at_x + line + 1 - 2 * even_x, line) - at_x)
    else:
        even_y, pair_y, pair_far = even_x, pair_x, pair_x
    foreign = (left, right, opp)
    pairs = (pair_x, pair_y, pair_far)
    sides = (even_x, even_y, even_x)
    fourth, eighth = width // 4, width // 8

    def w_rows(c, i, away=0, start=0, count=fourth):
        side = sides[i] if away == 0 else 1 - sides[i]
        return pl.ds(pl.multiple_of((2 * c + side) * fourth, fourth) + start, count)

    def w_give(src, dst, sem, to, line=me):
        return pltpu.make_async_remote_copy(
            src_ref=src, dst_ref=dst, send_sem=w_send.at[sem], recv_sem=w_recv.at[sem],
            device_id=(line, to), device_id_type=MESH,
        )

    def w_slice(rows_at, block):
        return w_out_hbm.at[rows_at, pl.ds(pl.multiple_of(block * depth, depth), depth)]

    def same(ref, sem):
        return w_give(ref, ref, sem, right)

    first_e, second_e = w_rows(core, 2, 0, 0, eighth), w_rows(core, 2, 0, eighth, eighth)
    w_near = [
        w_give(w_slice(first_e, opp), w_relay.at[0], 2, right),
        w_give(w_slice(second_e, opp), w_relay.at[1], 3, left),
        w_give(w_slice(w_rows(core, 0), right), w_cols.at[z, w_rows(core, 0)], 0, right),
        w_give(w_slice(w_rows(core, 1), left), w_cols.at[z, w_rows(core, 1)], 1, left),
    ]
    w_got = [
        same(w_relay.at[0], 2), same(w_relay.at[1], 3),
        same(w_cols.at[left, w_rows(core, 0)], 0), same(w_cols.at[right, w_rows(core, 1)], 1),
    ]
    w_fwd = [
        w_give(w_relay.at[0], w_cols.at[left, first_e], 4, right),
        w_give(w_relay.at[1], w_cols.at[right, second_e], 5, left),
    ]
    w_fwd_got = [same(w_cols.at[opp, first_e], 4), same(w_cols.at[opp, second_e], 5)]

    def w_pairs(away):
        refs = [w_cols.at[foreign[i], w_rows(core, i, away)] for i in range(3)]
        return [w_give(refs[i], refs[i], 6 + i, z, pairs[i]) for i in range(3)]

    def w_shares(c):
        refs = [w_cols.at[block, pl.ds(pl.multiple_of(c * 2 * fourth, fourth), 2 * fourth)] for block in foreign]
        return [w_give(refs[i], refs[i], 9 + i, z, sibling) for i in range(3)]

    w_pair, w_paired = w_pairs(0), w_pairs(1)
    w_share, w_theirs = w_shares(core), w_shares(1 - core)
    own_w = load(w_slice(pl.ds(0, width), z), w_cols.at[z], 6)
    own_w.start()

    def hop(buf, sems, block, at, sem, to):
        return pltpu.make_async_remote_copy(
            src_ref=buf.at[block, at], dst_ref=buf.at[block, at],
            send_sem=sems[0].at[sem], recv_sem=sems[1].at[sem],
            device_id=(me, to), device_id_type=MESH,
        )

    def full(span):
        return pl.ds(*span)

    def upper(span):
        return pl.ds(span[0], span[1] // 2)

    def lower(span):
        return pl.ds(span[0] + span[1] // 2, span[1] // 2)

    class Ring:
        def __init__(self, parts, buf, *sems):
            self.parts, self.buf, self.sems = parts, buf, sems
            self.started = []

        def start(self, *copies):
            for copy in copies:
                copy.start()
                self.started.append(copy)

        def copy(self, *what):
            return hop(self.buf, self.sems, *what)

        def own(self, c):
            self.start(self.copy(z, full(self.parts[c]), 4 * c, right), self.copy(z, full(self.parts[c]), 4 * c + 1, left))

        def near(self, c):
            self.copy(left, full(self.parts[c]), 4 * c, right).wait_recv()
            self.start(self.copy(left, upper(self.parts[c]), 4 * c + 2, right))
            self.copy(right, full(self.parts[c]), 4 * c + 1, left).wait_recv()
            self.start(self.copy(right, lower(self.parts[c]), 4 * c + 3, left))

        def far(self, c):
            self.copy(opp, upper(self.parts[c]), 4 * c + 2, right).wait_recv()
            self.copy(opp, lower(self.parts[c]), 4 * c + 3, left).wait_recv()

        def sent(self):
            for copy in self.started:
                copy.wait_send()

    tokens = Ring(chunks, feat, ag_send, ag_recv)
    for c in range(min(2, len(chunks))):
        tokens.own(c)

    def swap(src, dst, cols, sems, mine, theirs):
        where = () if cols is None else (slice(None), cols)
        return lambda peer: pltpu.make_async_remote_copy(
            src_ref=src.at[(mine, *where)], dst_ref=dst.at[(theirs, *where)],
            send_sem=x_send.at[sems], recv_sem=x_recv.at[sems],
            device_id=(peer, z), device_id_type=MESH,
        )

    def swap_start(src, dst, cols, sems):
        peers(lambda peer: swap(src, dst, cols, sems, peer, me)(peer).start())
        where = () if cols is None else (slice(None), cols)
        dst[(pl.ds(me, 1), *where)] = src[(pl.ds(me, 1), *where)]

    others = pl.ds(0, blocks - 1)

    def swap_arrived(*refs):
        swap(*refs, others, others)(me).wait_recv()

    def swap_sent(*refs):
        swap(*refs, others, others)(me).wait_send()

    h_refs = (hsend, hrecv, None, 0)
    spec_load.wait()
    for a in range(2):
        for ri in range(2):
            turned = mm_t(unit(width), spec[ri, a].astype(bf16)).astype(bf16)
            turned = mm(turned, unit(tok, 2 * me + a > blocks)).astype(bf16)
            hsend[:, ri, a] = turned.reshape(blocks, chans, tok)
    swap_start(*h_refs)

    def project(block, c, low=0, high=3):
        at = pl.ds(pl.multiple_of(block * depth, depth), depth)
        rows_at = full(chunks[c])

        @pl.loop(low, high)
        def _(g):
            acc[g, rows_at] += mm(feat[block, rows_at], w_in[g, at])

    w_loads[0].wait()
    own_at = pl.ds(pl.multiple_of(z * depth, depth), depth)

    @pl.loop(0, 3)
    def _(g):
        acc[g] = mm(feat[z], w_in[g, own_at])

    def s_refs(c):
        return sig, xrecv, full(chunks[c]), 1 + c

    def far_chunk(c):
        tokens.far(c)
        project(opp, c, 1, 3)
        rows_at = full(chunks[c])
        keys, values = acc[1, rows_at].astype(bf16), acc[2, rows_at].astype(bf16)
        signal = (keys.astype(f32) * values.astype(f32)).astype(bf16)
        turned = mm_t(unit(width), signal).astype(bf16)
        sig[:, :, rows_at] = turned.reshape(blocks, chans, chunks[c][1])
        swap_start(*s_refs(c))
        project(opp, c, 0, 1)

    final = len(chunks) - 1
    for c in range(final + 1):
        tokens.near(c)
        if c + 2 <= final:
            tokens.own(c + 2)
        if c == final:
            for copy in w_near:
                copy.start()
        if c == 0:
            w_loads[1].wait()
            w_loads[2].wait()
        project(left, c)
        project(right, c)
        if c == min(1, final):
            w_loads[3].wait()
        if c > 0:
            far_chunk(c - 1)
    far_chunk(final)
    qt[...] = mm_t(unit(width), acc[0].astype(bf16)).astype(bf16)

    swap_arrived(*h_refs)
    filt[:, 0] = hrecv[0, :, 0].astype(f32)
    filt[:, blocks] = hrecv[blocks // 2, :, 0].astype(f32)

    @pl.loop(1, blocks)
    def _(a):
        other = 2 * blocks - a
        near = hrecv[a // 2, :, a % 2].astype(f32)
        far = hrecv[other // 2, :, other % 2].astype(f32)
        filt[0, a] = near[0] + far[0]
        filt[1, a] = near[1] - far[1]

    for copy in rest:
        copy.wait()

    def at(a):
        return pl.ds(pl.multiple_of(a * chans, chans), chans)

    def outer_chunk(c):
        swap_arrived(*s_refs(c))
        start, count = chunks[c]
        cols = full(chunks[c])
        tmp[:, :count] = mm(first[...], xrecv[:, :, cols].reshape(blocks * chans, count))
        real, imag = pl.ds(2 * start, count), pl.ds(2 * start + count, count)

        @pl.loop(0, blocks + 1)
        def _(a):
            pr, pi = tmp[at(a), :count], tmp[at(blocks + 1 + a), :count]
            tc, ts = twist[0, a, :, cols], twist[1, a, :, cols]
            q[at(a), real] = (pr * tc + pi * ts).astype(bf16)
            q[at(a), imag] = (pi * tc - pr * ts).astype(bf16)

    early = 2 * chunks[final][0]
    for c in range(final):
        outer_chunk(c)
    if early:
        for i in range(2):
            part[i] = mm(q[:, :early], forward[:early, i * tok:(i + 1) * tok])
    for i in range(2):
        w_got[i].wait_recv()
        w_fwd[i].start()
    outer_chunk(final)
    for i in range(2):
        term = mm(q[:, early:], forward[early:, i * tok:(i + 1) * tok])
        part[i] = part[i] + term if early else term

    @pl.loop(0, blocks + 1)
    def _(a):
        xr, xi = part[0, at(a)], part[1, at(a)]
        hr, hi = filt[0, a], filt[1, a]
        q[at(a), :tok] = (xr * hr - xi * hi).astype(bf16)
        q[at(a), tok:] = (xr * hi + xi * hr).astype(bf16)

    def c_refs(c):
        return y, conv, full(outs[c]), 1 + len(chunks) + c

    for c, (start, count) in enumerate(outs):
        back[:, :2 * count] = mm(q[...], inverse[:, 2 * start:2 * (start + count)])
        cols = full(outs[c])

        @pl.loop(0, blocks + 1)
        def _(a):
            ur, ui = back[at(a), :count], back[at(a), count:2 * count]
            tc, ts = twist[0, a, :, cols], twist[1, a, :, cols]
            v[at(a), :count] = (ur * tc - ui * ts).astype(bf16)
            v[at(blocks + 1 + a), :count] = (ur * ts + ui * tc).astype(bf16)

        y[:, :, cols] = mm(last[...], v[:, :count]).astype(bf16).reshape(blocks, chans, count)
        swap_start(*c_refs(c))

    for i in range(2):
        w_got[2 + i].wait_recv()
        w_pair[i].start()

    rows_all = Ring(outs, gall, r_send, r_recv)

    def gate(c):
        swap_arrived(*c_refs(c))
        cols, count = full(outs[c]), outs[c][1]
        values = conv[:, :, cols].reshape(width, count).astype(f32)
        gated_t = (qt[:, cols].astype(f32) * values).astype(bf16)
        gall[pl.ds(z, 1), cols] = mm_t(unit(count), gated_t).astype(bf16)[None]
        rows_all.own(c)

    def term(block, c):
        return mm(gall[block, full(outs[c])], w_cols[block])

    ends = len(outs)
    for c in range(ends):
        gate(c)
        if c == 0:
            for got in w_fwd_got:
                got.wait_recv()
            w_pair[2].start()
        else:
            rows_all.near(c - 1)
    for i in range(3):
        w_paired[i].wait_recv()
        w_share[i].start()
    rows_all.near(ends - 1)
    own_w.wait()
    for c in range(ends):
        side[full(outs[c])] = term(z, c)
    w_theirs[0].wait_recv()
    w_theirs[1].wait_recv()
    for c in range(ends):
        side[full(outs[c])] += term(left, c) + term(right, c)
    w_theirs[2].wait_recv()
    outgoing = []
    for c in range(ends):
        rows_all.far(c)
        rows_at = full(outs[c])
        stage[rows_at] = (side[rows_at] + term(opp, c)).astype(bf16)
        outgoing.append(load(stage.at[rows_at], out_hbm.at[rows_at], 12 + c))
        outgoing[-1].start()

    for copy in outgoing:
        copy.wait()
    tokens.sent()
    rows_all.sent()
    for copy in w_near + w_fwd + w_pair + w_share:
        copy.wait_send()
    swap_sent(*h_refs)
    for c in range(final + 1):
        swap_sent(*s_refs(c))
    for c in range(ends):
        swap_sent(*c_refs(c))


def local(nz, blocks, tokens, w_in, w_out, spectra):
    tok, depth = tokens.shape
    width = w_in.shape[2]
    chans = width // blocks
    rows = (blocks + 1) * chans
    chunks, outs = spans(IN_PARTS, tok), spans(OUT_PARTS, tok)
    widest_in, widest_out = max(n for _, n in chunks), max(n for _, n in outs)
    consts = [jnp.asarray(t) for t in tables(blocks, tok, chans, chunks, outs)]
    dma = pltpu.SemaphoreType.DMA
    vmem = pltpu.VMEM
    scratch = [
        vmem((nz, tok, depth), bf16),
        vmem((3, nz * depth, width), bf16),
        vmem((nz, width, depth), bf16),
        vmem((2, width // 8, depth), bf16),
        vmem(spectra.shape, f32),
        *[vmem(t.shape, t.dtype) for t in consts],
        vmem((3, tok, width), f32),
        vmem((blocks, 2, 2, chans, tok), bf16),
        vmem((blocks, 2, 2, chans, tok), bf16),
        vmem((2, blocks + 1, chans, tok), f32),
        vmem((blocks, chans, tok), bf16),
        vmem((blocks, chans, tok), bf16),
        vmem((2 * rows, widest_in), f32),
        vmem((2, rows, tok), f32),
        vmem((rows, 2 * tok), bf16),
        vmem((rows, 2 * widest_out), f32),
        vmem((2 * rows, widest_out), bf16),
        vmem((blocks, chans, tok), bf16),
        vmem((blocks, chans, tok), bf16),
        vmem((width, tok), bf16),
        vmem((nz, tok, width), bf16),
        vmem((tok, depth), f32),
        vmem((tok, depth), bf16),
        dma((12 + len(outs),)),
        dma((4 * len(chunks),)), dma((4 * len(chunks),)),
        dma((1 + len(chunks) + len(outs),)), dma((1 + len(chunks) + len(outs),)),
        dma((4 * len(outs),)), dma((4 * len(outs),)),
        dma((12,)), dma((12,)),
    ]
    return pl.pallas_call(
        functools.partial(kernel, nz, blocks, tok, chans, chunks, outs),
        out_shape=jax.ShapeDtypeStruct((tok, depth), bf16),
        in_specs=[pl.BlockSpec(memory_space=pl.ANY)] * 9,
        out_specs=pl.BlockSpec(memory_space=pl.ANY),
        scratch_shapes=scratch,
        compiler_params=pltpu.CompilerParams(
            collective_id=0, has_side_effects=True, vmem_limit_bytes=62 * 1024 * 1024
        ),
    )(tokens, jnp.swapaxes(w_in, 0, 1), w_out, spectra, *consts)


def solution(mesh):
    in_specs = (P("seq", "ch"), P(None, None, "ch"), P("ch", None), P(None, "seq", None, "ch"))
    body = functools.partial(local, mesh.shape["ch"], mesh.shape["seq"])
    return jax.shard_map(body, mesh=mesh, in_specs=in_specs, out_specs=P("seq", "ch"), check_vma=False)
```

time: 96.9 us -> 85 us (0.88); the launches traced: 96.8 us -> 83.9 us
  Pallas kernels: 94.5 us -> 81.6 us
    pallas_call x1, Pallas kernels: 94.5 us -> 81.6 us  [local(): pl.pallas_call(functools.partial(kernel, nz, blocks, tok, chans, chunks,...]
where the time goes in v4:
time: 85 us; the launch traced here: 83.9 us
  Pallas kernels  81.6 us (96%)
  local copies, waits for them, and re-layouts  2.26 us (3%)
    pallas_call x1, Pallas kernels, local(): pl.pallas_call(functools.partial(kernel, nz, blocks, tok, chans, chunks,...  81.6 us
    unnamed x1, local copies, waits for them, and re-layouts  2.26 us

profile of v4, /device:TPU:1, one launch (start us, length us, event | category | flops | bytes accessed | tf_op | source)
XLA Modules:
  0.0 83.9 jit_solution(3511298658930278285)
XLA Ops:
  0.0 81.6 %shard_map.91 = bf16[512,1024]{1,0:T(8,128)(2,1)} custom-call(bf16[512,1024]{1,0:T(8,128)(2,1)} %tokens_hbm.1, bf16[3,4096,512]{2,1,0:T(8,128)(2,1)} %bitcast.1, bf16[512,4096]{1,0:T(8,128)(2,1)} %w_out_hbm.1, f32[2,2,512,512]{3,2,1,0:T(8,128)} %spectra_hbm.1, bf16[1056,512]{1,0:T(8,128)(2,1)} %constant.10.clone.first_hbm, ...), custom_call_target="tpu_custom_call" | custom-call | tf_op jit(solution)/shard_map/pallas_call | solution.py:476
  81.6 2.3 %copy.11 = bf16[512,1024]{1,0:T(8,128)(2,1)} copy(bf16[512,1024]{1,0:T(8,128)(2,1)} %shard_map.91) | data formatting | bytes 2097152

commit v5 on v4

--- a/solution.py
+++ b/solution.py
@@ -34,8 +34,9 @@
     def order(parts):
         return np.concatenate([np.arange(a, a + n) + i * tok for a, n in parts for i in range(2)])
 
-    forward = np.block([[c, -s], [s, c]])[order(chunks)]
-    inverse = np.block([[c, s], [-s, c]])[:, order(outs)]
+    tiles = order([(i, min(128, tok)) for i in range(0, tok, min(128, tok))])
+    forward = np.block([[c, -s], [s, c]])[order(chunks)][:, tiles]
+    inverse = np.block([[c, s], [-s, c]])[tiles][:, order(outs)]
     twist = 2 * np.pi * (freq[:, None] * pos[None, :]) / total
     twist = np.stack([np.cos(twist), np.sin(twist)])[:, :, None, :]
     return (
@@ -68,8 +69,8 @@
     tokens_hbm, w_in_hbm, w_out_hbm, spectra_hbm, first_hbm, last_hbm, forward_hbm, inverse_hbm, twist_hbm,
     out_hbm,
     feat, w_in, w_cols, w_relay, spec, first, last, forward, inverse, twist,
-    acc, hsend, hrecv, filt, sig, xrecv, tmp, part, q, back, v, y, conv, qt,
-    gall, side, stage,
+    acc, hsend, hrecv, filt, sig, xrecv, tmp, part, q, spec_prod, back, v, y, conv, qt,
+    gall, side, stage, eye,
     load_sem, ag_send, ag_recv, x_send, x_recv, r_send, r_recv, w_send, w_recv,
 ):
     me = lax.axis_index("seq")
@@ -78,6 +79,18 @@
     width = chans * blocks
     depth = tokens_hbm.shape[1]
 
+    barrier = pltpu.get_barrier_semaphore()
+    for near in (left, right):
+        pl.semaphore_signal(barrier, inc=1, device_id=(me, near), device_id_type=MESH)
+
+    def peers(act):
+        mid = blocks // 2
+        for low, high in ((mid, blocks), (blocks + 1, blocks + mid)):
+            @pl.loop(low, high, unroll=True)
+            def _(k):
+                act(lax.rem(me + k, blocks))
+
+    peers(lambda peer: pl.semaphore_signal(barrier, inc=1, device_id=(peer, z), device_id_type=MESH))
     def load(src, dst, sem):
         return pltpu.make_async_copy(src, dst, load_sem.at[sem])
 
@@ -97,18 +110,11 @@
     for copy in w_loads + rest:
         copy.start()
 
-    barrier = pltpu.get_barrier_semaphore()
-    for near in (left, right):
-        pl.semaphore_signal(barrier, inc=1, device_id=(me, near), device_id_type=MESH)
-
-    def peers(act):
-        mid = blocks // 2
-        for low, high in ((mid, blocks), (blocks + 1, blocks + mid)):
-            @pl.loop(low, high, unroll=True)
-            def _(k):
-                act(lax.rem(me + k, blocks))
-
-    peers(lambda peer: pl.semaphore_signal(barrier, inc=1, device_id=(peer, z), device_id_type=MESH))
+    eye[...] = unit(max(tok, width))
+
+    def same_size(n):
+        return eye[:n, :n]
+
     pl.semaphore_wait(barrier, blocks + 1)
     tok_load.wait()
 
@@ -250,7 +256,7 @@
     spec_load.wait()
     for a in range(2):
         for ri in range(2):
-            turned = mm_t(unit(width), spec[ri, a].astype(bf16)).astype(bf16)
+            turned = mm_t(same_size(width), spec[ri, a].astype(bf16)).astype(bf16)
             turned = mm(turned, unit(tok, 2 * me + a > blocks)).astype(bf16)
             hsend[:, ri, a] = turned.reshape(blocks, chans, tok)
     swap_start(*h_refs)
@@ -259,7 +265,7 @@
         at = pl.ds(pl.multiple_of(block * depth, depth), depth)
         rows_at = full(chunks[c])
 
-        @pl.loop(low, high)
+        @pl.loop(low, high, unroll=True)
         def _(g):
             acc[g, rows_at] += mm(feat[block, rows_at], w_in[g, at])
 
@@ -279,7 +285,7 @@
         rows_at = full(chunks[c])
         keys, values = acc[1, rows_at].astype(bf16), acc[2, rows_at].astype(bf16)
         signal = (keys.astype(f32) * values.astype(f32)).astype(bf16)
-        turned = mm_t(unit(width), signal).astype(bf16)
+        turned = mm_t(same_size(width), signal).astype(bf16)
         sig[:, :, rows_at] = turned.reshape(blocks, chans, chunks[c][1])
         swap_start(*s_refs(c))
         project(opp, c, 0, 1)
@@ -302,13 +308,13 @@
         if c > 0:
             far_chunk(c - 1)
     far_chunk(final)
-    qt[...] = mm_t(unit(width), acc[0].astype(bf16)).astype(bf16)
+    qt[...] = mm_t(same_size(width), acc[0].astype(bf16)).astype(bf16)
 
     swap_arrived(*h_refs)
     filt[:, 0] = hrecv[0, :, 0].astype(f32)
     filt[:, blocks] = hrecv[blocks // 2, :, 0].astype(f32)
 
-    @pl.loop(1, blocks)
+    @pl.loop(1, blocks, unroll=True)
     def _(a):
         other = 2 * blocks - a
         near = hrecv[a // 2, :, a % 2].astype(f32)
@@ -329,7 +335,7 @@
         tmp[:, :count] = mm(first[...], xrecv[:, :, cols].reshape(blocks * chans, count))
         real, imag = pl.ds(2 * start, count), pl.ds(2 * start + count, count)
 
-        @pl.loop(0, blocks + 1)
+        @pl.loop(0, blocks + 1, unroll=True)
         def _(a):
             pr, pi = tmp[at(a), :count], tmp[at(blocks + 1 + a), :count]
             tc, ts = twist[0, a, :, cols], twist[1, a, :, cols]
@@ -340,31 +346,31 @@
     for c in range(final):
         outer_chunk(c)
     if early:
-        for i in range(2):
-            part[i] = mm(q[:, :early], forward[:early, i * tok:(i + 1) * tok])
+        part[...] = mm(q[:, :early], forward[:early])
     for i in range(2):
         w_got[i].wait_recv()
         w_fwd[i].start()
     outer_chunk(final)
-    for i in range(2):
-        term = mm(q[:, early:], forward[early:, i * tok:(i + 1) * tok])
-        part[i] = part[i] + term if early else term
-
-    @pl.loop(0, blocks + 1)
-    def _(a):
-        xr, xi = part[0, at(a)], part[1, at(a)]
-        hr, hi = filt[0, a], filt[1, a]
-        q[at(a), :tok] = (xr * hr - xi * hi).astype(bf16)
-        q[at(a), tok:] = (xr * hi + xi * hr).astype(bf16)
+    tile = min(128, tok)
+    for i in range(0, tok, tile):
+        both = pl.ds(2 * i, 2 * tile)
+        x = mm(q[:, early:], forward[early:, 2 * i:2 * (i + tile)])
+        if early:
+            x += part[:, both]
+        x = x.reshape(blocks + 1, chans, 2 * tile)
+        xr, xi = x[..., :tile], x[..., tile:]
+        hr, hi = filt[0, :, :, i:i + tile], filt[1, :, :, i:i + tile]
+        prod = jnp.concatenate([xr * hr - xi * hi, xr * hi + xi * hr], axis=2)
+        spec_prod[:, both] = prod.astype(bf16).reshape((blocks + 1) * chans, 2 * tile)
 
     def c_refs(c):
         return y, conv, full(outs[c]), 1 + len(chunks) + c
 
     for c, (start, count) in enumerate(outs):
-        back[:, :2 * count] = mm(q[...], inverse[:, 2 * start:2 * (start + count)])
+        back[:, :2 * count] = mm(spec_prod[...], inverse[:, 2 * start:2 * (start + count)])
         cols = full(outs[c])
 
-        @pl.loop(0, blocks + 1)
+        @pl.loop(0, blocks + 1, unroll=True)
         def _(a):
             ur, ui = back[at(a), :count], back[at(a), count:2 * count]
             tc, ts = twist[0, a, :, cols], twist[1, a, :, cols]
@@ -385,7 +391,7 @@
         cols, count = full(outs[c]), outs[c][1]
         values = conv[:, :, cols].reshape(width, count).astype(f32)
         gated_t = (qt[:, cols].astype(f32) * values).astype(bf16)
-        gall[pl.ds(z, 1), cols] = mm_t(unit(count), gated_t).astype(bf16)[None]
+        gall[pl.ds(z, 1), cols] = mm_t(same_size(count), gated_t).astype(bf16)[None]
         rows_all.own(c)
 
     def term(block, c):
@@ -457,7 +463,8 @@
         vmem((blocks, chans, tok), bf16),
         vmem((blocks, chans, tok), bf16),
         vmem((2 * rows, widest_in), f32),
-        vmem((2, rows, tok), f32),
+        vmem((rows, 2 * tok), f32),
+        vmem((rows, 2 * tok), bf16),
         vmem((rows, 2 * tok), bf16),
         vmem((rows, 2 * widest_out), f32),
         vmem((2 * rows, widest_out), bf16),
@@ -467,6 +474,7 @@
         vmem((nz, tok, width), bf16),
         vmem((tok, depth), f32),
         vmem((tok, depth), bf16),
+        vmem((max(tok, width),) * 2, bf16),
         dma((12 + len(outs),)),
         dma((4 * len(chunks),)), dma((4 * len(chunks),)),
         dma((1 + len(chunks) + len(outs),)), dma((1 + len(chunks) + len(outs),)),

time: 85 us -> 82.9 us (0.975)
  Pallas kernels: 81.6 us -> 79.5 us
    pallas_call x1, Pallas kernels: 81.6 us -> 79.5 us  [local(): pl.pallas_call(functools.partial(kernel, nz, blocks, tok, chans, chunks,...]
where the time goes in v5:
time: 82.9 us; the launch traced here: 81.8 us
  Pallas kernels  79.5 us (96%)
  local copies, waits for them, and re-layouts  2.26 us (3%)
    pallas_call x1, Pallas kernels, local(): pl.pallas_call(functools.partial(kernel, nz, blocks, tok, chans, chunks,...  79.5 us
    unnamed x1, local copies, waits for them, and re-layouts  2.26 us

profile of v5, /device:TPU:1, one launch (start us, length us, event | category | flops | bytes accessed | tf_op | source)
XLA Modules:
  0.0 81.8 jit_solution(13343060841639915667)
XLA Ops:
  0.0 79.5 %shard_map.91 = bf16[512,1024]{1,0:T(8,128)(2,1)} custom-call(bf16[512,1024]{1,0:T(8,128)(2,1)} %tokens_hbm.1, bf16[3,4096,512]{2,1,0:T(8,128)(2,1)} %bitcast.1, bf16[512,4096]{1,0:T(8,128)(2,1)} %w_out_hbm.1, f32[2,2,512,512]{3,2,1,0:T(8,128)} %spectra_hbm.1, bf16[1056,512]{1,0:T(8,128)(2,1)} %constant.10.clone.first_hbm, ...), custom_call_target="tpu_custom_call" | custom-call | tf_op jit(solution)/shard_map/pallas_call | solution.py:484
  79.5 2.3 %copy.11 = bf16[512,1024]{1,0:T(8,128)(2,1)} copy(bf16[512,1024]{1,0:T(8,128)(2,1)} %shard_map.91) | data formatting | bytes 2097152

commit v6 on v5

--- a/solution.py
+++ b/solution.py
@@ -115,6 +115,17 @@
     def same_size(n):
         return eye[:n, :n]
 
+    def h_refs(a):
+        return hsend, hrecv, a, a
+
+    def turn_filter(a):
+        for ri in range(2):
+            turned = mm_t(same_size(width), spec[ri, a].astype(bf16)).astype(bf16)
+            turned = mm(turned, unit(tok, 2 * me + a > blocks)).astype(bf16)
+            hsend[:, ri, a] = turned.reshape(blocks, chans, tok)
+
+    spec_load.wait()
+    turn_filter(0)
     pl.semaphore_wait(barrier, blocks + 1)
     tok_load.wait()
 
@@ -232,7 +243,7 @@
         tokens.own(c)
 
     def swap(src, dst, cols, sems, mine, theirs):
-        where = () if cols is None else (slice(None), cols)
+        where = (slice(None), cols)
         return lambda peer: pltpu.make_async_remote_copy(
             src_ref=src.at[(mine, *where)], dst_ref=dst.at[(theirs, *where)],
             send_sem=x_send.at[sems], recv_sem=x_recv.at[sems],
@@ -241,7 +252,7 @@
 
     def swap_start(src, dst, cols, sems):
         peers(lambda peer: swap(src, dst, cols, sems, peer, me)(peer).start())
-        where = () if cols is None else (slice(None), cols)
+        where = (slice(None), cols)
         dst[(pl.ds(me, 1), *where)] = src[(pl.ds(me, 1), *where)]
 
     others = pl.ds(0, blocks - 1)
@@ -252,14 +263,9 @@
     def swap_sent(*refs):
         swap(*refs, others, others)(me).wait_send()
 
-    h_refs = (hsend, hrecv, None, 0)
-    spec_load.wait()
-    for a in range(2):
-        for ri in range(2):
-            turned = mm_t(same_size(width), spec[ri, a].astype(bf16)).astype(bf16)
-            turned = mm(turned, unit(tok, 2 * me + a > blocks)).astype(bf16)
-            hsend[:, ri, a] = turned.reshape(blocks, chans, tok)
-    swap_start(*h_refs)
+    swap_start(*h_refs(0))
+    turn_filter(1)
+    swap_start(*h_refs(1))
 
     def project(block, c, low=0, high=3):
         at = pl.ds(pl.multiple_of(block * depth, depth), depth)
@@ -277,7 +283,7 @@
         acc[g] = mm(feat[z], w_in[g, own_at])
 
     def s_refs(c):
-        return sig, xrecv, full(chunks[c]), 1 + c
+        return sig, xrecv, full(chunks[c]), 2 + c
 
     def far_chunk(c):
         tokens.far(c)
@@ -310,7 +316,8 @@
     far_chunk(final)
     qt[...] = mm_t(same_size(width), acc[0].astype(bf16)).astype(bf16)
 
-    swap_arrived(*h_refs)
+    swap_arrived(*h_refs(0))
+    swap_arrived(*h_refs(1))
     filt[:, 0] = hrecv[0, :, 0].astype(f32)
     filt[:, blocks] = hrecv[blocks // 2, :, 0].astype(f32)
 
@@ -364,7 +371,7 @@
         spec_prod[:, both] = prod.astype(bf16).reshape((blocks + 1) * chans, 2 * tile)
 
     def c_refs(c):
-        return y, conv, full(outs[c]), 1 + len(chunks) + c
+        return y, conv, full(outs[c]), 2 + len(chunks) + c
 
     for c, (start, count) in enumerate(outs):
         back[:, :2 * count] = mm(spec_prod[...], inverse[:, 2 * start:2 * (start + count)])
@@ -418,6 +425,17 @@
     for c in range(ends):
         side[full(outs[c])] += term(left, c) + term(right, c)
     w_theirs[2].wait_recv()
+
+    tokens.sent()
+    for copy in w_near + w_fwd + w_pair + w_share:
+        copy.wait_send()
+    swap_sent(*h_refs(0))
+    swap_sent(*h_refs(1))
+    for c in range(final + 1):
+        swap_sent(*s_refs(c))
+    for c in range(ends):
+        swap_sent(*c_refs(c))
+
     outgoing = []
     for c in range(ends):
         rows_all.far(c)
@@ -426,17 +444,9 @@
         outgoing.append(load(stage.at[rows_at], out_hbm.at[rows_at], 12 + c))
         outgoing[-1].start()
 
+    rows_all.sent()
     for copy in outgoing:
         copy.wait()
-    tokens.sent()
-    rows_all.sent()
-    for copy in w_near + w_fwd + w_pair + w_share:
-        copy.wait_send()
-    swap_sent(*h_refs)
-    for c in range(final + 1):
-        swap_sent(*s_refs(c))
-    for c in range(ends):
-        swap_sent(*c_refs(c))
 
 
 def local(nz, blocks, tokens, w_in, w_out, spectra):
@@ -477,7 +487,7 @@
         vmem((max(tok, width),) * 2, bf16),
         dma((12 + len(outs),)),
         dma((4 * len(chunks),)), dma((4 * len(chunks),)),
-        dma((1 + len(chunks) + len(outs),)), dma((1 + len(chunks) + len(outs),)),
+        dma((2 + len(chunks) + len(outs),)), dma((2 + len(chunks) + len(outs),)),
         dma((4 * len(outs),)), dma((4 * len(outs),)),
         dma((12,)), dma((12,)),
     ]

time: 82.9 us -> 83.1 us (level)
  no operation moved by 1% of the time
where the time goes in v6:
time: 83.1 us; the launch traced here: 82.1 us
  Pallas kernels  79.8 us (96%)
  local copies, waits for them, and re-layouts  2.26 us (3%)
    pallas_call x1, Pallas kernels, local(): pl.pallas_call(functools.partial(kernel, nz, blocks, tok, chans, chunks,...  79.8 us
    unnamed x1, local copies, waits for them, and re-layouts  2.26 us

profile of v6, /device:TPU:1, one launch (start us, length us, event | category | flops | bytes accessed | tf_op | source)
XLA Modules:
  0.0 82.1 jit_solution(10372373584454355036)
XLA Ops:
  0.0 79.8 %shard_map.91 = bf16[512,1024]{1,0:T(8,128)(2,1)} custom-call(bf16[512,1024]{1,0:T(8,128)(2,1)} %tokens_hbm.1, bf16[3,4096,512]{2,1,0:T(8,128)(2,1)} %bitcast.1, bf16[512,4096]{1,0:T(8,128)(2,1)} %w_out_hbm.1, f32[2,2,512,512]{3,2,1,0:T(8,128)} %spectra_hbm.1, bf16[1056,512]{1,0:T(8,128)(2,1)} %constant.10.clone.first_hbm, ...), custom_call_target="tpu_custom_call" | custom-call | tf_op jit(solution)/shard_map/pallas_call | solution.py:494
  79.8 2.3 %copy.11 = bf16[512,1024]{1,0:T(8,128)(2,1)} copy(bf16[512,1024]{1,0:T(8,128)(2,1)} %shard_map.91) | data formatting | bytes 2097152
